TPU v7x, 512 devices: a whole 4x8x8 slice. The times are simulated.
512 devices in a mesh: phys: 2 (over core), sta: 64 (over z, y), cell: 4 (over x).
Axes of the slice: x: 4, y: 8, z: 8, core: 2. Of those that a mesh axis runs over, the one named last changes fastest.
Arguments:
- sensitivity: float32 [2, 1024, 131072], P('phys', 'sta', 'cell'), may hold values from -60 to 60, as said below
- observed: float32 [2, 1024], P('phys', 'sta'), may hold values from -6 to 6
- data_weight: float32 [2, 1024], P('phys', 'sta'), may hold values from 0.3 to 3
- phys_weight: float32 [2], P('phys'), may hold values from 0.5 to 2
- start_model: float32 [131072], P('cell'), may hold values from -6 to 6
Outputs:
- cell_weight: float32 [4, 32768], P('cell', 'sta')
- gradient: float32 [4, 32768], P('cell', 'sta')
- final_model: float32 [4, 32768], P('cell', 'sta')
Inputs may be any that keep to these rules, and one draw needn't show every extreme that they name: `sensitivity`: dense, full rank sensitivities.
All inputs are finite; a program needn't handle non-finite values.
Results may differ from a plain program's by a relative error of at most 0.0003.
Values sent between devices are 32-bit elements; how exact they have to be, the bound alone decides.
No kernel may reach another device: no remote copies, remote signals or barrier semaphores. Data moves between devices by JAX's collectives and lax.ppermute only.
A program may use at most 64 MiB of HBM per device.

v0:
```python
import math

import jax
import jax.numpy as jnp
from jax import lax
from jax.sharding import PartitionSpec as P

ITERS = 2


step_size = 0.5
weight_floor = 0.1
epsilon = 1e-06


def per_device(sensitivity, observed, data_weight, phys_weight, start_model):
    highest = lax.Precision.HIGHEST
    sta_count = lax.axis_size("sta")
    cell_count = sensitivity.shape[2]
    share_len = cell_count // sta_count
    position = lax.axis_index("sta")
    physics = sensitivity.shape[0] * lax.axis_size("phys")
    root_cells = math.sqrt(cell_count * lax.axis_size("cell"))
    root_stations = math.sqrt(sensitivity.shape[1] * sta_count)
    weight_sq = data_weight * data_weight
    column = jnp.einsum("ps,psc->pc", weight_sq, sensitivity * sensitivity, precision=highest)
    model_full = start_model
    gradient_full = jnp.zeros_like(start_model)
    column_full = lax.psum(column, "sta")
    column_max = lax.pmax(jnp.max(column_full, axis=1), "cell")
    relative = jnp.sqrt(column_full / (column_max[:, None] + epsilon))
    weight_flat = weight_floor + lax.psum(jnp.sum(relative, axis=0), "phys") / physics
    first_step = 0
    for step_index in range(first_step, ITERS):
        local_pred = jnp.einsum("psc,c->ps", sensitivity, model_full, precision=highest)
        predicted = lax.psum(local_pred, "cell") / root_cells
        residual = data_weight * (predicted - observed)
        weighted = phys_weight[:, None] * data_weight * residual
        partial_value = jnp.einsum("psc,ps->c", sensitivity, weighted, precision=highest)
        summed = lax.psum(lax.psum(partial_value, "sta"), "phys")
        gradient_full = summed / (root_stations * weight_flat)
        model_full = model_full - step_size * gradient_full
    weight_out = lax.dynamic_slice_in_dim(weight_flat, position * share_len, share_len)
    gradient_out = lax.dynamic_slice_in_dim(gradient_full, position * share_len, share_len)
    model_out = lax.dynamic_slice_in_dim(model_full, position * share_len, share_len)
    return (
        weight_out.reshape(1, share_len),
        gradient_out.reshape(1, share_len),
        model_out.reshape(1, share_len),
    )


def solution(mesh):
    return jax.shard_map(
        per_device,
        mesh=mesh,
        in_specs=(
            P("phys", "sta", "cell"),
            P("phys", "sta"),
            P("phys", "sta"),
            P("phys"),
            P("cell"),
        ),
        out_specs=(P("cell", "sta"), P("cell", "sta"), P("cell", "sta")),
        check_vma=False,
    )
```

profile of v0, /device:TPU:1, one launch (start us, length us, event | category | flops | bytes accessed | tf_op | source)
XLA Modules:
  0.0 435.9 jit_solution(5398213615637577158)
XLA Ops:
  7.2 0.0 copy-start
  7.2 0.0 copy-start.3
  7.2 0.0 all-reduce.11.cloned.1.call-start
  8.0 0.0 copy-start.4
  8.0 4.2 fusion.6
  12.2 9.3 %psum.58 = f32[1,16]{1,0:T(1,128)S(1)} all-reduce(f32[1,16]{1,0:T(1,128)S(1)} %fusion.6), channel_id=1, replica_groups=mesh['phys'=2,'sta'=64,'cell'=4] {'cell'}, use_global_device_ids=true, to_apply=%region_4.0 | all-reduce | flops 16 | bytes 128 | tf_op jit(solution)/shard_map/psum | solution.py:36
  21.5 0.0 copy-done
  21.5 0.0 copy-done.3
  21.5 1.9 fusion.8
  23.4 0.0 copy-done.4
  23.4 1.8 fusion.4
  25.1 0.0 all-reduce.11.cloned.1.call-update
  25.2 0.0 all-reduce.13.cloned.1.call-start
  25.2 152.6 %all-reduce.11.cloned.1.call-done = (f32[1,32768]{1,0:T(1,128)}, f32[32768]{0:T(1024)}) async-done(((f32[1,32768]{1,0:T(1,128)}, f32[32768]{0:T(1024)}), (f32[1,32768]{1,0:T(1,128)}, f32[32768]{0:T(1024)})) %all-reduce.11.cloned.1.call-update) | async-done | bytes 262160 | tf_op jit(solution)/shard_map/psum | solution.py:29
  177.8 1.8 reduce_max.11
  179.6 9.0 %pmax.7 = f32[1]{0:T(128)} all-reduce(f32[1]{0:T(128)} %bitcast.4), channel_id=1, replica_groups=mesh['phys'=2,'sta'=64,'cell'=4] {'cell'}, use_global_device_ids=true, to_apply=%region_2.0 | all-reduce | flops 1 | bytes 8 | tf_op jit(solution)/shard_map/pmax | solution.py:30
  189.2 1.8 divide_sqrt_fusion
  191.1 0.0 all-reduce.13.cloned.1.call-update
  191.1 0.0 all-reduce.7.cloned.1.call-start
  191.1 36.8 %all-reduce.13.cloned.1.call-done = (f32[32768]{0:T(1024)}, f32[32768]{0:T(1024)}) async-done(((f32[32768]{0:T(1024)}, f32[32768]{0:T(1024)}), (f32[32768]{0:T(1024)}, f32[32768]{0:T(1024)})) %all-reduce.13.cloned.1.call-update) | async-done | bytes 262160 | tf_op jit(solution)/shard_map/psum | solution.py:32
  227.9 1.0 multiply_subtract_fusion
  228.9 2.5 fusion.2
  231.4 7.4 %psum.61 = f32[1,16]{1,0:T(1,128)S(1)} all-reduce(f32[1,16]{1,0:T(1,128)S(1)} %fusion.2), channel_id=1, replica_groups=mesh['phys'=2,'sta'=64,'cell'=4] {'cell'}, use_global_device_ids=true, to_apply=%region_7.0 | all-reduce | flops 16 | bytes 128 | tf_op jit(solution)/shard_map/psum | solution.py:36
  238.8 1.8 fusion
  240.6 0.0 all-reduce.7.cloned.1.call-update
  240.6 0.0 all-reduce.9.cloned.1.call-start
  240.7 147.2 %all-reduce.7.cloned.1.call-done = f32[32768]{0:T(1024)} async-done(((f32[32768]{0:T(1024)}), f32[32768]{0:T(1024)}) %all-reduce.7.cloned.1.call-update) | async-done | bytes 131088 | tf_op jit(solution)/shard_map/psum | solution.py:40
  387.8 0.0 all-reduce.9.cloned.1.call-update
  387.9 39.2 %all-reduce.9.cloned.1.call-done = f32[32768]{0:T(1024)} async-done(((f32[32768]{0:T(1024)}), f32[32768]{0:T(1024)}) %all-reduce.9.cloned.1.call-update) | async-done | bytes 131088 | tf_op jit(solution)/shard_map/psum | solution.py:40
  427.1 0.9 multiply_divide_fusion
  428.0 0.7 dynamic-slice_subtract_fusion
  428.7 0.7 dynamic_slice.9
  (4 shorter events, 0.0 us)
Async XLA Ops:
  7.2 14.3 %copy-start = (f32[1,16,32768]{2,1,0:T(8,128)S(1)}, f32[1,16,32768]{2,1,0:T(8,128)}, u32[]{:S(2)}) copy-start(f32[1,16,32768]{2,1,0:T(8,128)} %param.5) | copy-start | bytes 6291460
  7.2 14.3 %copy-start.3 = (f32[1,16]{1,0:T(1,128)S(1)}, f32[1,16]{1,0:T(1,128)}, u32[]{:S(2)}) copy-start(f32[1,16]{1,0:T(1,128)} %param.7) | copy-start | bytes 196
  7.2 170.6 %all-reduce.11.cloned.1.call-start = ((), (), s32[]{:S(2)}) async-start(), calls=%async_computation.2 | async-start | bytes 524288 | tf_op jit(solution)/shard_map/psum | solution.py:29
  8.0 15.4 %copy-start.4 = (f32[1,16]{1,0:T(1,128)S(1)}, f32[1,16]{1,0:T(1,128)}, u32[]{:S(2)}) copy-start(f32[1,16]{1,0:T(1,128)} %param.6) | copy-start | bytes 196
  23.4 204.6 %copy-start.1 = (f32[32768]{0:T(1024)S(1)}, f32[32768]{0:T(1024)}, u32[]{:S(2)}) copy-start(f32[32768]{0:T(1024)} %param.9) | copy-start | bytes 393220
  25.2 202.8 %all-reduce.13.cloned.1.call-start = ((), (), s32[]{:S(2)}) async-start(), calls=%async_computation.3 | async-start | bytes 524288 | tf_op jit(solution)/shard_map/psum | solution.py:32
  191.1 196.7 %all-reduce.7.cloned.1.call-start = ((), (), s32[]{:S(2)}) async-start(), calls=%async_computation | async-start | bytes 262144 | tf_op jit(solution)/shard_map/psum | solution.py:40
  228.9 198.2 %copy-start.2 = (f32[32768]{0:T(1024)S(1)}, f32[32768]{0:T(1024)}, u32[]{:S(2)}) copy-start(f32[32768]{0:T(1024)} %get-tuple-element.5) | copy-start | bytes 393220
  240.6 186.5 %all-reduce.9.cloned.1.call-start = ((), (), s32[]{:S(2)}) async-start(), calls=%async_computation.1 | async-start | bytes 262144 | tf_op jit(solution)/shard_map/psum | solution.py:40
Sparse Core Ops, SparseCore 0:
  25.3 152.4 all-reduce.10
  191.2 36.6 all-reduce.12
  240.8 147.0 all-reduce.6
  390.8 36.2 all-reduce.8
where the time goes:
time: 436 us
  waiting for transfers between devices  376 us (86%)
  blocking collectives  25.7 us (6%)
  between operations  15.2 us (3%)
  matrix products  12.1 us (3%)
  other arithmetic  6.22 us (1%)
    psum x2, waiting for transfers between devices, per_device(): summed = lax.psum(lax.psum(partial_value, 'sta'), 'phys')  186 us
    psum x1, waiting for transfers between devices, per_device(): column_full = lax.psum(column, 'sta')  153 us
    psum x1, waiting for transfers between devices, per_device(): lax.psum(jnp.sum(relative, axis=0), 'phys') / physics  36.8 us
    psum x2, blocking collectives, per_device(): predicted = lax.psum(local_pred, 'cell') / root_cells  16.7 us
    pmax x1, blocking collectives, per_device(): column_max = lax.pmax(jnp.max(column_full, axis=1), 'cell')  9.01 us
  transfers between devices with their start and end apart: 4, of which 4 were waited for; matrix products, arithmetic and copies ran while one was open for 0% of the time, Pallas kernels for 0%

commit v1 on v0

v1 whole, which is shorter than its diff:
```python
import math

import jax
import jax.numpy as jnp
from jax import lax
from jax.sharding import PartitionSpec as P

ITERS = 2
LANES = 128

step_size = 0.5
weight_floor = 0.1
epsilon = 1e-06


def per_device(sensitivity, observed, data_weight, phys_weight, start_model):
    highest = lax.Precision.HIGHEST
    sta_count = lax.axis_size("sta")
    cell_blocks = lax.axis_size("cell")
    phys_count = lax.axis_size("phys")
    cell_count = sensitivity.shape[2]
    rows = cell_count // sta_count // LANES
    physics = sensitivity.shape[0] * phys_count
    root_cells = math.sqrt(cell_count * cell_blocks)
    root_stations = math.sqrt(sensitivity.shape[1] * sta_count)
    sens = sensitivity[0]
    weight_sq = data_weight * data_weight
    position = lax.axis_index("sta")
    cell_at = lax.axis_index("cell")

    def slices(vector):
        return vector.reshape(sta_count, rows, LANES)

    def gradient_terms(local_pred):
        predicted = lax.psum(local_pred, "cell") / root_cells
        residual = data_weight * (predicted - observed)
        weighted = phys_weight[:, None] * data_weight * residual
        return slices(jnp.einsum("sc,ps->pc", sens, weighted, precision=highest))

    def to_owners(terms):
        return jnp.sum(lax.all_to_all(terms, "sta", 0, 0, tiled=True), axis=0)

    column_terms = slices(jnp.einsum("ps,sc->pc", weight_sq, sens * sens, precision=highest))
    first_terms = gradient_terms(jnp.einsum("sc,c->s", sens, start_model, precision=highest)[None])
    own = to_owners(jnp.concatenate([column_terms, first_terms], axis=1))
    both = lax.all_to_all(
        jnp.broadcast_to(own[None], (phys_count * cell_blocks,) + own.shape), ("phys", "cell"), 0, 0, tiled=True
    ).reshape(phys_count, cell_blocks, 2 * rows, LANES)
    slice_max = jnp.max(both[:, :, :rows], axis=(1, 2, 3))
    mine = lax.dynamic_index_in_dim(both, cell_at, axis=1, keepdims=False)
    message = jnp.concatenate(
        [
            mine[:, :rows].reshape(phys_count * rows, LANES),
            jnp.sum(mine[:, rows:], axis=0),
            jnp.broadcast_to(slice_max[:, None], (phys_count, LANES)),
        ],
        axis=0,
    )
    message = jnp.pad(message, ((0, 16 - message.shape[0]), (0, 0)))
    gathered = lax.all_to_all(
        jnp.broadcast_to(message[None], (sta_count,) + message.shape), "sta", 0, 0, tiled=True
    )
    column = gathered[:, : phys_count * rows].reshape(sta_count, phys_count, rows, LANES)
    first_summed = gathered[:, phys_count * rows : (phys_count + 1) * rows]
    max_at = (phys_count + 1) * rows
    column_max = jnp.max(gathered[:, max_at : max_at + phys_count], axis=(0, 2))
    relative = jnp.sqrt(column / (column_max[None, :, None, None] + epsilon))
    weight = weight_floor + jnp.sum(relative, axis=1) / physics
    model = slices(start_model) - step_size * (first_summed / (root_stations * weight))

    second_terms = gradient_terms(jnp.einsum("sc,c->s", sens, model.reshape(cell_count), precision=highest)[None])
    second = to_owners(second_terms)
    second_summed = jnp.sum(lax.all_gather(second, "phys"), axis=0)
    weight_own = lax.dynamic_index_in_dim(weight, position, keepdims=False)
    model_own = lax.dynamic_index_in_dim(model, position, keepdims=False)
    gradient = second_summed / (root_stations * weight_own)
    final = model_own - step_size * gradient
    return weight_own.reshape(1, -1), gradient.reshape(1, -1), final.reshape(1, -1)


def solution(mesh):
    return jax.shard_map(
        per_device,
        mesh=mesh,
        in_specs=(
            P("phys", "sta", "cell"),
            P("phys", "sta"),
            P("phys", "sta"),
            P("phys"),
            P("cell"),
        ),
        out_specs=(P("cell", "sta"), P("cell", "sta"), P("cell", "sta")),
        check_vma=False,
    )
```

time: 436 us -> 132 us (0.30)
  waiting for transfers between devices: 376 us -> 16.4 us
  blocking collectives: 25.7 us -> 72.2 us
  between operations: 15.2 us -> 1.41 us
  starting transfers between devices: 0.16 us -> 13.9 us
  local copies, waits for them, and re-layouts: 0.67 us -> 6.93 us
    psum x4 -> x0, waiting for transfers between devices: 376 us -> none  [the longest x2 186 us: per_device(): summed = lax.psum(lax.psum(partial_value, 'sta'), 'phys')]
    all_to_all x0 -> x2, blocking collectives: none -> 50.4 us  [the longest x1 28.7 us: to_owners(): return jnp.sum(lax.all_to_all(terms, 'sta', 0, 0, tiled=True), axis=0)]
    all_to_all x0 -> x2, waiting for transfers between devices: none -> 16.4 us  [the longest x1 11.5 us: to_owners(): return jnp.sum(lax.all_to_all(terms, 'sta', 0, 0, tiled=True), axis=0)]
    all_to_all x0 -> x2, starting transfers between devices: none -> 13.9 us  [the longest x1 7.31 us: per_device(): lax.all_to_all(jnp.broadcast_to(own[None], (phys_count * cell_blocks,) +...]
    pmax x1 -> x0, blocking collectives: 9.01 us -> none  [per_device(): column_max = lax.pmax(jnp.max(column_full, axis=1), 'cell')]
    dot_general x0 -> x2, local copies, waits for them, and re-layouts: none -> 6.14 us  [the longest x1 3.68 us: per_device(): jnp.einsum('ps,sc->pc', weight_sq, sens * sens, precision=highest)]
    all_gather x0 -> x1, blocking collectives: none -> 6.12 us  [per_device(): second_summed = jnp.sum(lax.all_gather(second, 'phys'), axis=0)]
  transfers between devices with their start and end apart: 4 -> 2, of which waited for: 4 -> 2; matrix products, arithmetic and copies ran while one was open for 0% -> 0% of each run, Pallas kernels for 0% -> 0%
where the time goes in v1:
time: 132 us; the launch traced here: 131 us
  blocking collectives  72.2 us (55%)
  waiting for transfers between devices  16.4 us (12%)
  matrix products  15.6 us (12%)
  starting transfers between devices  13.9 us (11%)
  local copies, waits for them, and re-layouts  6.93 us (5%)
  other arithmetic  4.71 us (4%)
  between operations  1.41 us (1%)
    all_to_all x1, blocking collectives, to_owners(): return jnp.sum(lax.all_to_all(terms, 'sta', 0, 0, tiled=True), axis=0)  28.7 us
    all_to_all x1, blocking collectives, per_device(): lax.all_to_all(jnp.broadcast_to(message[None], (sta_count,) + message.sha...  21.7 us
    psum x2, blocking collectives, gradient_terms(): predicted = lax.psum(local_pred, 'cell') / root_cells  15.6 us
    all_to_all x1, waiting for transfers between devices, to_owners(): return jnp.sum(lax.all_to_all(terms, 'sta', 0, 0, tiled=True), axis=0)  11.5 us
    all_to_all x1, starting transfers between devices, per_device(): lax.all_to_all(jnp.broadcast_to(own[None], (phys_count * cell_blocks,) +...  7.31 us
    dot_general x2, matrix products, gradient_terms(): return slices(jnp.einsum('sc,ps->pc', sens, weighted, precision=highest))  6.66 us
    all_to_all x1, starting transfers between devices, to_owners(): return jnp.sum(lax.all_to_all(terms, 'sta', 0, 0, tiled=True), axis=0)  6.6 us
    all_gather x1, blocking collectives, per_device(): second_summed = jnp.sum(lax.all_gather(second, 'phys'), axis=0)  6.12 us
  transfers between devices with their start and end apart: 2, of which 2 were waited for; matrix products, arithmetic and copies ran while one was open for 0% of the time, Pallas kernels for 0%

profile of v1, /device:TPU:1, one launch (start us, length us, event | category | flops | bytes accessed | tf_op | source)
XLA Modules:
  0.0 131.2 jit_solution(5830070281189230677)
XLA Ops:
  0.6 0.0 copy-start
  0.6 3.2 %fusion.4 = f32[32768,16]{0,1:T(8,128)} fusion(f32[1,16,32768]{2,1,0:T(8,128)} %param.5), kind=kLoop, calls=%fused_computation.5 | loop fusion | flops 524288 | bytes 4194304 | tf_op jit(solution)/shard_map/ps,sc->pc/dot_general | solution.py:43
  3.8 0.0 copy-done
  3.8 2.5 %dot_general.28 = f32[64,4,128,16]{2,1,0,3:T(4,128)} reshape(f32[32768,16]{0,1:T(8,128)S(1)} %bitcast.64) | data formatting | bytes 4194304 | tf_op jit(solution)/shard_map/sc,ps->pc/dot_general | solution.py:38
  6.3 2.6 %fusion.2 = f32[1,16]{1,0:T(1,128)S(1)} fusion(f32[32768,1]{0,1:T(1,128)S(1)} %bitcast.67, f32[1,16,32768]{2,1,0:T(8,128)S(1)} %copy-done), kind=kOutput, calls=%fused_computation.2 | convolution fusion | flops 6291456 | bytes 2228288 | tf_op jit(solution)/shard_map/sc,c->s/dot_general | solution.py:44
  8.9 9.3 %psum.14 = f32[1,16]{1,0:T(1,128)S(1)} all-reduce(f32[1,16]{1,0:T(1,128)S(1)} %fusion.2), channel_id=1, replica_groups=mesh['phys'=2,'sta'=64,'cell'=4] {'cell'}, use_global_device_ids=true, to_apply=%region_0.0 | all-reduce | flops 16 | bytes 128 | tf_op jit(solution)/shard_map/psum | solution.py:35
  18.8 0.0 copy-start.4
  18.8 3.7 %dot_general.24 = f32[64,4,128,16]{2,1,0,3:T(4,128)} reshape(f32[32768,16]{0,1:T(8,128)} %fusion.4) | data formatting | bytes 4194304 | tf_op jit(solution)/shard_map/ps,sc->pc/dot_general | solution.py:43
  22.5 3.9 %fusion.5 = f32[1,64,4,128]{3,0,2,1:T(1,128)S(1)} fusion(f32[64,4,128,16]{2,1,0,3:T(4,128)} %dot_general.24, f32[1,16]{1,0:T(1,128)S(1)} %copy-done.4), kind=kOutput, calls=%fused_computation.6 | convolution fusion | flops 6291472 | bytes 2228288 | tf_op jit(solution)/shard_map/ps,sc->pc/dot_general | solution.py:43
  26.4 2.2 %fusion.9 = f32[1,64,4,128]{3,0,2,1:T(1,128)S(1)} fusion(f32[64,4,128,16]{2,1,0,3:T(4,128)S(1)} %copy-done.1, f32[1,16]{1,0:T(1,128)S(1)} %copy-done.4, f32[1,16]{1,0:T(1,128)S(1)} %copy-done.5, f32[1,16]{1,0:T(1,128)S(1)} %psum.14, f32[]{:T(128)} %bitcast.62), kind=kOutput, calls=%fused_computation.10 | convolution fusion | flops 6291536 | bytes 2228420 | tf_op jit(solution)/shard_map/sc,ps->pc/dot_general | solution.py:38
  28.7 0.1 pad_maximum_fusion
  28.7 28.7 %all_to_all.20 = f32[64,8,128]{2,1,0:T(8,128)S(1)} all-to-all(f32[64,8,128]{2,1,0:T(8,128)S(1)} %pad_maximum_fusion), channel_id=1, replica_groups=mesh['phys'=2,'sta'=64,'cell'=4] {'sta'}, dimensions={0} | all-to-all | bytes 524288 | tf_op jit(solution)/shard_map/all_to_all | solution.py:41
  57.4 0.1 reduce_sum.47
  57.5 0.6 broadcast_in_dim.11
  58.1 7.3 %all-to-all-start.1 = ((f32[8,8,128]{2,1,0:T(8,128)}), f32[8,8,128]{2,1,0:T(8,128)S(1)}, u32[]{:S(2)}, u32[]{:S(2)}) async-start(f32[8,8,128]{2,1,0:T(8,128)} %broadcast_in_dim.11), calls=%async_computation.1 | async-start | bytes 65536 | tf_op jit(solution)/shard_map/all_to_all | solution.py:46
  65.4 4.9 %all-to-all-done.1 = f32[8,8,128]{2,1,0:T(8,128)S(1)} async-done(((f32[8,8,128]{2,1,0:T(8,128)}), f32[8,8,128]{2,1,0:T(8,128)S(1)}, u32[]{:S(2)}, u32[]{:S(2)}) %all-to-all-start.1) | async-done | bytes 32800 | tf_op jit(solution)/shard_map/all_to_all | solution.py:46
  70.3 0.1 slice_reduce_fusion.1
  70.5 0.1 pad.7.clone
  70.5 0.1 maximum_maximum_fusion
  70.7 21.7 %all_to_all.21 = f32[64,16,128]{2,1,0:T(8,128)S(1)} all-to-all(f32[64,16,128]{2,1,0:T(8,128)S(1)} %broadcast_in_dim.13), channel_id=1, replica_groups=mesh['phys'=2,'sta'=64,'cell'=4] {'sta'}, dimensions={0} | all-to-all | bytes 1048576 | tf_op jit(solution)/shard_map/all_to_all | solution.py:60
  92.4 0.2 slice_reduce_fusion
  92.6 0.3 sqrt_reduce_fusion
  92.9 0.1 multiply_subtract_fusion
  93.0 2.5 %fusion = f32[1,16]{1,0:T(1,128)S(1)} fusion(f32[32768,1]{0,1:T(1,128)S(1)} %bitcast.66, f32[1,16,32768]{2,1,0:T(8,128)S(1)} %copy-done), kind=kOutput, calls=%fused_computation | convolution fusion | flops 6291456 | bytes 2228288 | tf_op jit(solution)/shard_map/sc,c->s/dot_general | solution.py:71
  95.4 6.4 %psum.15 = f32[1,16]{1,0:T(1,128)S(1)} all-reduce(f32[1,16]{1,0:T(1,128)S(1)} %fusion), channel_id=1, replica_groups=mesh['phys'=2,'sta'=64,'cell'=4] {'cell'}, use_global_device_ids=true, to_apply=%region_6.7 | all-reduce | flops 16 | bytes 128 | tf_op jit(solution)/shard_map/psum | solution.py:35
  101.8 4.4 %fusion.7 = f32[1,64,4,128]{3,0,2,1:T(1,128)} fusion(f32[64,4,128,16]{2,1,0,3:T(4,128)} %dot_general.28, f32[1,16]{1,0:T(1,128)S(1)} %copy-done.4, f32[1,16]{1,0:T(1,128)S(1)} %copy-done.5, f32[1,16]{1,0:T(1,128)S(1)} %psum.15, f32[]{:T(128)} %bitcast.63), kind=kOutput, calls=%fused_computation.8 | convolution fusion | flops 6291536 | bytes 2228420 | tf_op jit(solution)/shard_map/sc,ps->pc/dot_general | solution.py:38
  106.2 6.6 %all-to-all-start.3 = ((f32[64,4,128]{2,1,0:T(4,128)}), f32[64,4,128]{2,1,0:T(4,128)S(1)}, u32[]{:S(2)}, u32[]{:S(2)}) async-start(f32[64,4,128]{2,1,0:T(4,128)} %bitcast.29), calls=%async_computation.3 | async-start | bytes 262144 | tf_op jit(solution)/shard_map/all_to_all | solution.py:41
  112.9 0.0 copy-start.3
  112.9 11.5 %all-to-all-done.3 = f32[64,4,128]{2,1,0:T(4,128)S(1)} async-done(((f32[64,4,128]{2,1,0:T(4,128)}), f32[64,4,128]{2,1,0:T(4,128)S(1)}, u32[]{:S(2)}, u32[]{:S(2)}) %all-to-all-start.3) | async-done | bytes 131104 | tf_op jit(solution)/shard_map/all_to_all | solution.py:41
  124.4 0.1 reduce_sum.50
  124.5 6.1 %all-gather.1 = f32[2,4,128]{2,1,0:T(4,128)S(1)} all-gather(f32[1,4,128]{2,1,0:T(4,128)S(1)} %bitcast.74), channel_id=2, replica_groups=mesh['phys'=2,'sta'=64,'cell'=4] {'phys'}, dimensions={0}, use_global_device_ids=true | all-gather | bytes 6144 | tf_op jit(solution)/shard_map/all_gather | solution.py:73
  130.6 0.6 multiply_subtract_fusion.1
  (16 shorter events, 0.1 us)
Async XLA Ops:
  0.6 3.2 %copy-start = (f32[1,16,32768]{2,1,0:T(8,128)S(1)}, f32[1,16,32768]{2,1,0:T(8,128)}, u32[]{:S(2)}) copy-start(f32[1,16,32768]{2,1,0:T(8,128)} %param.5) | copy-start | bytes 6291460
  3.8 2.5 %copy-start.2 = (f32[32768]{0:T(1024)S(1)}, f32[32768]{0:T(1024)}, u32[]{:S(2)}) copy-start(f32[32768]{0:T(1024)} %param.9) | copy-start | bytes 393220
  18.8 3.7 %copy-start.4 = (f32[1,16]{1,0:T(1,128)S(1)}, f32[1,16]{1,0:T(1,128)}, u32[]{:S(2)}) copy-start(f32[1,16]{1,0:T(1,128)} %param.7) | copy-start | bytes 196
  22.5 3.9 %copy-start.1 = (f32[64,4,128,16]{2,1,0,3:T(4,128)S(1)}, f32[64,4,128,16]{2,1,0,3:T(4,128)}, u32[]{:S(2)}) copy-start(f32[64,4,128,16]{2,1,0,3:T(4,128)} %dot_general.28) | copy-start | bytes 6291460
  22.5 3.9 %copy-start.5 = (f32[1,16]{1,0:T(1,128)S(1)}, f32[1,16]{1,0:T(1,128)}, u32[]{:S(2)}) copy-start(f32[1,16]{1,0:T(1,128)} %param.6) | copy-start | bytes 196
  58.1 12.2 %all-to-all-start.1 = ((f32[8,8,128]{2,1,0:T(8,128)}), f32[8,8,128]{2,1,0:T(8,128)S(1)}, u32[]{:S(2)}, u32[]{:S(2)}) async-start(f32[8,8,128]{2,1,0:T(8,128)} %broadcast_in_dim.11), calls=%async_computation.1 | async-start | bytes 65536 | tf_op jit(solution)/shard_map/all_to_all | solution.py:46
  106.2 18.2 %all-to-all-start.3 = ((f32[64,4,128]{2,1,0:T(4,128)}), f32[64,4,128]{2,1,0:T(4,128)S(1)}, u32[]{:S(2)}, u32[]{:S(2)}) async-start(f32[64,4,128]{2,1,0:T(4,128)} %bitcast.29), calls=%async_computation.3 | async-start | bytes 262144 | tf_op jit(solution)/shard_map/all_to_all | solution.py:41
  112.9 18.3 %copy-start.3 = (f32[1,4,128]{2,1,0:T(4,128)}, f32[1,4,128]{2,1,0:T(4,128)S(1)}, u32[]{:S(2)}) copy-start(f32[1,4,128]{2,1,0:T(4,128)S(1)} %get-tuple-element.10) | copy-start | bytes 6148

commit v2 on v0

v2 whole, which is shorter than its diff:
```python
import functools
import math

import jax
import jax.numpy as jnp
from jax import lax
from jax.experimental import pallas as pl
from jax.experimental.pallas import tpu as pltpu
from jax.sharding import PartitionSpec as P

ITERS = 2
LANES = 128
SUB = 8

step_size = 0.5
weight_floor = 0.1
epsilon = 1e-06

VMEM = pl.BlockSpec(memory_space=pltpu.VMEM)


def chunk(sens, half, at):
    return sens[half * SUB : (half + 1) * SUB, pl.ds(at * LANES, LANES)]


def predict(sens, model, halves):
    chunks = model.shape[0]

    def body(step, acc):
        acc = list(acc)
        for k in range(SUB):
            at = step * SUB + k
            row = model[pl.ds(at, 1), :]
            for half in range(halves):
                slot = (k % 4) * halves + half
                acc[slot] = acc[slot] + chunk(sens, half, at) * row
        return tuple(acc)

    zero = jnp.zeros((SUB, LANES), jnp.float32)
    acc = lax.fori_loop(0, chunks // SUB, body, (zero,) * (4 * halves), unroll=2)
    return [
        (acc[half] + acc[halves + half]) + (acc[2 * halves + half] + acc[3 * halves + half])
        for half in range(halves)
    ]


def as_column(row, halves):
    stations = SUB * halves
    wide = jnp.broadcast_to(row, (stations, stations))
    at = lax.broadcasted_iota(jnp.int32, (stations, stations), 0)
    to = lax.broadcasted_iota(jnp.int32, (stations, stations), 1)
    column = jnp.sum(jnp.where(at == to, wide, 0.0), axis=1, keepdims=True)
    return [column[half * SUB : (half + 1) * SUB] for half in range(halves)]


def weighted_residual(parts, observed, data_weight, phys_weight, halves, root_cells):
    total = parts[0]
    for block in range(1, parts.shape[0]):
        total = total + parts[block]
    predicted = jnp.sum(total, axis=1, keepdims=True) / root_cells
    seen = as_column(observed[...], halves)
    weight = as_column(data_weight[...], halves)
    scale = phys_weight[0, 0]
    weighted = []
    for half in range(halves):
        residual = weight[half] * (predicted[half * SUB : (half + 1) * SUB] - seen[half])
        weighted.append(scale * weight[half] * residual)
    return weight, weighted


def predict_kernel(sens, model, out):
    halves = sens.shape[0] // SUB
    acc = predict(sens, model, halves)
    for block in range(out.shape[0]):
        for half in range(halves):
            out[block, half * SUB : (half + 1) * SUB, :] = acc[half]


def first_terms_kernel(root_cells, parts, sens, observed, data_weight, phys_weight, out):
    halves = sens.shape[0] // SUB
    rows = out.shape[1] // 2
    weight, weighted = weighted_residual(parts, observed, data_weight, phys_weight, halves, root_cells)
    wide = [jnp.broadcast_to(w, (SUB, LANES)) for w in weighted]
    square = [jnp.broadcast_to(w * w, (SUB, LANES)) for w in weight]

    def body(owner, carry):
        for row in range(rows):
            column = gradient = None
            for half in range(halves):
                block = chunk(sens, half, owner * rows + row)
                c = block * block * square[half]
                g = block * wide[half]
                column = c if column is None else column + c
                gradient = g if gradient is None else gradient + g
            out[owner, row : row + 1, :] = jnp.sum(column, axis=0, keepdims=True)
            out[owner, rows + row : rows + row + 1, :] = jnp.sum(gradient, axis=0, keepdims=True)
        return carry

    lax.fori_loop(0, out.shape[0], body, 0, unroll=2)


def second_terms_kernel(root_cells, parts, sens, observed, data_weight, phys_weight, out):
    halves = sens.shape[0] // SUB
    rows = out.shape[1]
    _, weighted = weighted_residual(parts, observed, data_weight, phys_weight, halves, root_cells)
    wide = [jnp.broadcast_to(w, (SUB, LANES)) for w in weighted]

    def body(owner, carry):
        for row in range(rows):
            gradient = None
            for half in range(halves):
                g = chunk(sens, half, owner * rows + row) * wide[half]
                gradient = g if gradient is None else gradient + g
            out[owner, row : row + 1, :] = jnp.sum(gradient, axis=0, keepdims=True)
        return carry

    lax.fori_loop(0, out.shape[0], body, 0, unroll=4)


def sum_leading(ref):
    return jnp.sum(ref[...], axis=0)


def owner_sum_kernel(received, out):
    total = sum_leading(received)
    for peer in range(out.shape[0]):
        out[peer] = total


def message_kernel(rows, cell_blocks, both, out):
    phys_count = both.shape[0] // cell_blocks
    cell_at = lax.axis_index("cell")
    gradient = None
    pieces, largest = [], []
    for method in range(phys_count):
        block = both[method * cell_blocks + cell_at]
        pieces.append(block[:rows])
        gradient = block[rows:] if gradient is None else gradient + block[rows:]
        most = both[method * cell_blocks, :rows]
        for other in range(1, cell_blocks):
            most = jnp.maximum(most, both[method * cell_blocks + other, :rows])
        largest.append(jnp.max(most, axis=0, keepdims=True))
    used = rows * (phys_count + 1) + phys_count
    fill = jnp.zeros((out.shape[1] - used, LANES), jnp.float32)
    tile = jnp.concatenate(pieces + [gradient] + largest + [fill], axis=0)

    def body(peer, carry):
        out[peer] = tile
        return carry

    lax.fori_loop(0, out.shape[0], body, 0, unroll=8)


def model_kernel(rows, phys_count, physics, root_stations, message, start, sens, parts, own, model):
    owners = message.shape[0]
    position = lax.axis_index("sta")
    max_at = rows * (phys_count + 1)
    most = jnp.max(message[:, max_at : max_at + phys_count, :], axis=0)
    most = jnp.max(most, axis=1, keepdims=True)
    scales = 1.0 / (most + epsilon)

    def weights(owner):
        relative = None
        for method in range(phys_count):
            column = message[owner, method * rows : (method + 1) * rows, :]
            r = jnp.sqrt(column * scales[method : method + 1])
            relative = r if relative is None else relative + r
        return weight_floor + relative / physics

    def stepped(owner, weight):
        summed = message[owner, phys_count * rows : (phys_count + 1) * rows, :]
        return start[owner] - step_size * (summed / (root_stations * weight))

    def body(owner, carry):
        model[pl.ds(owner * rows, rows), :] = stepped(owner, weights(owner))
        return carry

    lax.fori_loop(0, owners, body, 0, unroll=4)
    weight_own = weights(position)
    own[0] = weight_own
    own[1] = stepped(position, weight_own)
    halves = sens.shape[0] // SUB
    acc = predict(sens, model, halves)
    for block in range(parts.shape[0]):
        for half in range(halves):
            parts[block, half * SUB : (half + 1) * SUB, :] = acc[half]


def second_sum_kernel(received, out):
    out[...] = sum_leading(received)


def final_kernel(root_stations, summed, own, weight_out, gradient_out, model_out):
    total = sum_leading(summed)
    weight = own[0]
    gradient = total / (root_stations * weight)
    model = own[1] - step_size * gradient
    for row in range(total.shape[0]):
        lanes = slice(row * LANES, (row + 1) * LANES)
        weight_out[:, lanes] = weight[row : row + 1]
        gradient_out[:, lanes] = gradient[row : row + 1]
        model_out[:, lanes] = model[row : row + 1]


def kernel_call(kernel, name, outs, operands, scratch=(), flops=0):
    out_shape = [jax.ShapeDtypeStruct(s, jnp.float32) for s in outs]
    return pl.pallas_call(
        kernel,
        name=name,
        out_shape=out_shape,
        in_specs=[VMEM] * len(operands),
        out_specs=[VMEM] * len(outs),
        scratch_shapes=scratch,
        compiler_params=pltpu.CompilerParams(vmem_limit_bytes=16 * 2**20),
    )(*operands)


def per_device(sensitivity, observed, data_weight, phys_weight, start_model):
    sta_count = lax.axis_size("sta")
    cell_blocks = lax.axis_size("cell")
    phys_count = lax.axis_size("phys")
    stations, cell_count = sensitivity.shape[1:]
    rows = cell_count // sta_count // LANES
    physics = sensitivity.shape[0] * phys_count
    root_cells = math.sqrt(cell_count * cell_blocks)
    root_stations = math.sqrt(stations * sta_count)
    sens = sensitivity.reshape(stations, cell_count)
    start_rows = start_model.reshape(cell_count // LANES, LANES)
    start_slices = start_model.reshape(sta_count, rows, LANES)
    scale = phys_weight.reshape(1, 1)
    message_rows = -(-(rows * (phys_count + 1) + phys_count) // SUB) * SUB

    def swap(array, axes):
        return lax.all_to_all(array, axes, 0, 0, tiled=True)

    parts_shape = (cell_blocks, stations, LANES)
    (parts,) = kernel_call(predict_kernel, "predict", [parts_shape], [sens, start_rows])
    parts = swap(parts, "cell")
    (terms,) = kernel_call(
        functools.partial(first_terms_kernel, root_cells),
        "first_terms",
        [(sta_count, 2 * rows, LANES)],
        [parts, sens, observed, data_weight, scale],
    )
    terms = swap(terms, "sta")
    peers = phys_count * cell_blocks
    (both,) = kernel_call(owner_sum_kernel, "owner_sum", [(peers, 2 * rows, LANES)], [terms])
    both = swap(both, ("phys", "cell"))
    (message,) = kernel_call(
        functools.partial(message_kernel, rows, cell_blocks),
        "message",
        [(sta_count, message_rows, LANES)],
        [both],
    )
    message = swap(message, "sta")
    parts, own = kernel_call(
        functools.partial(model_kernel, rows, phys_count, physics, root_stations),
        "model",
        [parts_shape, (2, rows, LANES)],
        [message, start_slices, sens],
        scratch=[pltpu.VMEM((cell_count // LANES, LANES), jnp.float32)],
    )
    parts = swap(parts, "cell")
    (terms,) = kernel_call(
        functools.partial(second_terms_kernel, root_cells),
        "second_terms",
        [(sta_count, rows, LANES)],
        [parts, sens, observed, data_weight, scale],
    )
    terms = swap(terms, "sta")
    (summed,) = kernel_call(second_sum_kernel, "second_sum", [(rows, LANES)], [terms])
    summed = lax.all_gather(summed, "phys")
    out = (1, rows * LANES)
    return tuple(kernel_call(functools.partial(final_kernel, root_stations), "final", [out] * 3, [summed, own]))


def solution(mesh):
    return jax.shard_map(
        per_device,
        mesh=mesh,
        in_specs=(
            P("phys", "sta", "cell"),
            P("phys", "sta"),
            P("phys", "sta"),
            P("phys"),
            P("cell"),
        ),
        out_specs=(P("cell", "sta"), P("cell", "sta"), P("cell", "sta")),
        check_vma=False,
    )
```

time: 436 us -> 108 us (0.25)
  waiting for transfers between devices: 376 us -> 3.65 us
  blocking collectives: 25.7 us -> 90.7 us
  between operations: 15.2 us -> 1.36 us
  matrix products: 12.1 us -> 0 us
  other arithmetic: 6.22 us -> 0 us
  starting transfers between devices: 0.16 us -> 4.84 us
    psum x4 -> x0, waiting for transfers between devices: 376 us -> none  [the longest x2 186 us: per_device(): summed = lax.psum(lax.psum(partial_value, 'sta'), 'phys')]
    all_to_all x0 -> x5, blocking collectives: none -> 85.5 us  [swap(): return lax.all_to_all(array, axes, 0, 0, tiled=True)]
    psum x2 -> x0, blocking collectives: 16.7 us -> none  [per_device(): predicted = lax.psum(local_pred, 'cell') / root_cells]
    dot_general x5 -> x0, matrix products: 12.1 us -> none  [the longest x2 6.66 us: per_device(): jnp.einsum('psc,c->ps', sensitivity, model_full, precision=highest)]
    pmax x1 -> x0, blocking collectives: 9.01 us -> none  [per_device(): column_max = lax.pmax(jnp.max(column_full, axis=1), 'cell')]
    all_gather x0 -> x1, blocking collectives: none -> 5.24 us  [per_device(): summed = lax.all_gather(summed, 'phys')]
    all_to_all x0 -> x1, starting transfers between devices: none -> 4.84 us  [swap(): return lax.all_to_all(array, axes, 0, 0, tiled=True)]
  transfers between devices with their start and end apart: 4 -> 1, of which waited for: 4 -> 1; matrix products, arithmetic and copies ran while one was open for 0% -> 0% of each run, Pallas kernels for 0% -> 0%
where the time goes in v2:
time: 108 us; the launch traced here: 107 us
  blocking collectives  90.7 us (84%)
  starting transfers between devices  4.84 us (4%)
  Pallas kernels  4.26 us (4%)
  waiting for transfers between devices  3.65 us (3%)
  local copies, waits for them, and re-layouts  2.52 us (2%)
  between operations  1.36 us (1%)
    all_to_all x5, blocking collectives, swap(): return lax.all_to_all(array, axes, 0, 0, tiled=True)  85.5 us
    all_gather x1, blocking collectives, per_device(): summed = lax.all_gather(summed, 'phys')  5.24 us
    all_to_all x1, starting transfers between devices, swap(): return lax.all_to_all(array, axes, 0, 0, tiled=True)  4.84 us
    pallas_call x8, Pallas kernels, kernel_call(): pl.pallas_call(kernel, name=name, out_shape=out_shape, in_specs=[VMEM] *...  4.26 us
    all_to_all x1, waiting for transfers between devices, swap(): return lax.all_to_all(array, axes, 0, 0, tiled=True)  3.65 us
    unnamed x12, local copies, waits for them, and re-layouts  2.52 us
  transfers between devices with their start and end apart: 1, of which 1 were waited for; matrix products, arithmetic and copies ran while one was open for 0% of the time, Pallas kernels for 0%

profile of v2, /device:TPU:1, one launch (start us, length us, event | category | flops | bytes accessed | tf_op | source)
XLA Modules:
  0.0 107.4 jit_solution(9046096740840074208)
XLA Ops:
  0.6 0.0 copy-start.5
  0.6 0.0 copy-start.4
  0.7 0.0 copy-start
  0.7 1.6 %copy-done = f32[1,16,32768]{2,1,0:T(8,128)S(1)} copy-done((f32[1,16,32768]{2,1,0:T(8,128)S(1)}, f32[1,16,32768]{2,1,0:T(8,128)}, u32[]{:S(2)}) %copy-start) | copy-done | bytes 2097176
  2.3 0.0 copy-start.2
  2.3 0.9 copy-done.2
  3.2 0.0 copy-start.1
  3.2 1.0 predict.1
  4.1 4.8 %all-to-all-start = ((f32[4,16,128]{2,1,0:T(8,128)}), f32[4,16,128]{2,1,0:T(8,128)S(1)}, u32[]{:S(2)}, u32[]{:S(2)}) async-start(f32[4,16,128]{2,1,0:T(8,128)} %predict.1), calls=%async_computation | async-start | bytes 65536 | tf_op jit(solution)/shard_map/all_to_all | solution.py:234
  9.6 3.6 %all-to-all-done.parts = f32[4,16,128]{2,1,0:T(8,128)S(1)} async-done(((f32[4,16,128]{2,1,0:T(8,128)}), f32[4,16,128]{2,1,0:T(8,128)S(1)}, u32[]{:S(2)}, u32[]{:S(2)}) %all-to-all-start) | async-done | bytes 32800 | tf_op jit(solution)/shard_map/all_to_all | solution.py:234
  13.3 0.0 copy-done.5
  13.3 0.0 copy-done.4
  13.3 0.0 copy-done.1
  13.3 0.0 copy-start.3
  13.3 1.0 first_terms.1
  14.3 28.6 %all_to_all.30.received = f32[64,8,128]{2,1,0:T(8,128)S(1)} all-to-all(f32[64,8,128]{2,1,0:T(8,128)S(1)} %first_terms.1), channel_id=1, replica_groups=mesh['phys'=2,'sta'=64,'cell'=4] {'sta'}, dimensions={0} | all-to-all | bytes 524288 | tf_op jit(solution)/shard_map/all_to_all | solution.py:234
  42.9 0.1 owner_sum.1
  43.0 10.8 %all_to_all.31.both = f32[8,8,128]{2,1,0:T(8,128)S(1)} all-to-all(f32[8,8,128]{2,1,0:T(8,128)S(1)} %owner_sum.1), channel_id=1, replica_groups=mesh['phys'=2,'sta'=64,'cell'=4] {'phys','cell'}, dimensions={0} | all-to-all | bytes 65536 | tf_op jit(solution)/shard_map/all_to_all | solution.py:234
  53.8 0.1 message.1
  53.9 21.6 %all_to_all.32.message = f32[64,16,128]{2,1,0:T(8,128)S(1)} all-to-all(f32[64,16,128]{2,1,0:T(8,128)S(1)} %message.1), channel_id=1, replica_groups=mesh['phys'=2,'sta'=64,'cell'=4] {'sta'}, dimensions={0} | all-to-all | bytes 1048576 | tf_op jit(solution)/shard_map/all_to_all | solution.py:234
  75.5 0.0 copy-done.3
  75.5 0.9 model.1
  76.5 6.7 %all_to_all.33.parts = f32[4,16,128]{2,1,0:T(8,128)S(1)} all-to-all(f32[4,16,128]{2,1,0:T(8,128)S(1)} %get-tuple-element.5), channel_id=1, replica_groups=mesh['phys'=2,'sta'=64,'cell'=4] {'cell'}, dimensions={0} | all-to-all | bytes 65536 | tf_op jit(solution)/shard_map/all_to_all | solution.py:234
  83.1 0.5 second_terms.1
  83.7 17.8 %all_to_all.34.received = f32[64,4,128]{2,1,0:T(4,128)S(1)} all-to-all(f32[64,4,128]{2,1,0:T(4,128)S(1)} %second_terms.1), channel_id=1, replica_groups=mesh['phys'=2,'sta'=64,'cell'=4] {'sta'}, dimensions={0} | all-to-all | bytes 262144 | tf_op jit(solution)/shard_map/all_to_all | solution.py:234
  101.5 0.1 second_sum.1
  101.5 5.2 %all-gather.1.summed = f32[2,4,128]{2,1,0:T(4,128)S(1)} all-gather(f32[1,4,128]{2,1,0:T(4,128)S(1)} %bitcast.13), channel_id=2, replica_groups=mesh['phys'=2,'sta'=64,'cell'=4] {'phys'}, dimensions={0}, use_global_device_ids=true | all-gather | bytes 6144 | tf_op jit(solution)/shard_map/all_gather | solution.py:272
  106.8 0.6 final.1
Async XLA Ops:
  0.6 12.7 %copy-start.5 = (f32[1,16]{1,0:T(1,128)S(1)}, f32[1,16]{1,0:T(1,128)}, u32[]{:S(2)}) copy-start(f32[1,16]{1,0:T(1,128)} %data_weight.3) | copy-start | bytes 196
  0.6 12.6 %copy-start.4 = (f32[1,16]{1,0:T(1,128)S(1)}, f32[1,16]{1,0:T(1,128)}, u32[]{:S(2)}) copy-start(f32[1,16]{1,0:T(1,128)} %observed.3) | copy-start | bytes 196
  0.7 1.6 %copy-start = (f32[1,16,32768]{2,1,0:T(8,128)S(1)}, f32[1,16,32768]{2,1,0:T(8,128)}, u32[]{:S(2)}) copy-start(f32[1,16,32768]{2,1,0:T(8,128)} %param.5) | copy-start | bytes 6291460
  2.3 0.9 copy-start.2
  3.2 10.1 %copy-start.1 = (f32[1,16,32768]{2,1,0:T(8,128)S(1)}, f32[1,16,32768]{2,1,0:T(8,128)}, u32[]{:S(2)}) copy-start(f32[1,16,32768]{2,1,0:T(8,128)} %param.5) | copy-start | bytes 6291460
  4.1 9.1 %all-to-all-start = ((f32[4,16,128]{2,1,0:T(8,128)}), f32[4,16,128]{2,1,0:T(8,128)S(1)}, u32[]{:S(2)}, u32[]{:S(2)}) async-start(f32[4,16,128]{2,1,0:T(8,128)} %predict.1), calls=%async_computation | async-start | bytes 65536 | tf_op jit(solution)/shard_map/all_to_all | solution.py:234
  13.3 62.2 %copy-start.3 = (f32[32768]{0:T(1024)S(1)}, f32[32768]{0:T(1024)}, u32[]{:S(2)}) copy-start(f32[32768]{0:T(1024)} %param.9) | copy-start | bytes 393220

commit v3 on v2

v3 whole, which is shorter than its diff:
```python
import functools
import math

import jax
import jax.numpy as jnp
from jax import lax
from jax.experimental import pallas as pl
from jax.experimental.pallas import tpu as pltpu
from jax.sharding import PartitionSpec as P

ITERS = 2
LANES = 128
SUB = 8

step_size = 0.5
weight_floor = 0.1
epsilon = 1e-06

def chunk(sens, half, at):
    return sens[half * SUB : (half + 1) * SUB, pl.ds(at * LANES, LANES)]


def predict(sens, model, halves, first, count, acc):
    def body(step, acc):
        acc = list(acc)
        for k in range(SUB):
            at = first + step * SUB + k
            row = model[pl.ds(at, 1), :]
            for half in range(halves):
                slot = (k % 4) * halves + half
                acc[slot] = acc[slot] + chunk(sens, half, at) * row
        return tuple(acc)

    return lax.fori_loop(0, count // SUB, body, acc, unroll=2)


def predict_start(halves):
    return (jnp.zeros((SUB, LANES), jnp.float32),) * (4 * halves)


def predict_store(acc, halves, out):
    for half in range(halves):
        total = (acc[half] + acc[halves + half]) + (acc[2 * halves + half] + acc[3 * halves + half])
        for block in range(out.shape[0]):
            out[block, half * SUB : (half + 1) * SUB, :] = total


def as_column(row):
    stations = row.shape[1]
    wide = jnp.broadcast_to(row, (stations, stations))
    at = lax.broadcasted_iota(jnp.int32, (stations, stations), 0)
    to = lax.broadcasted_iota(jnp.int32, (stations, stations), 1)
    column = jnp.sum(jnp.where(at == to, wide, 0.0), axis=1, keepdims=True)
    return jnp.broadcast_to(column, (stations, LANES))


def weighted_residual(parts, station, root_cells):
    total = parts[0]
    for block in range(1, parts.shape[0]):
        total = total + parts[block]
    predicted = jnp.sum(total, axis=1, keepdims=True) / root_cells
    weight, observed, scaled = station[0], station[1], station[2]
    residual = weight * (predicted - observed)
    return weight, scaled * residual


def predict_kernel(
    sens_hbm, model_hbm, observed_hbm, weight_hbm, scale, out, sens, station, model, observed, weight, sems
):
    halves, pieces = sens.shape[0] // SUB, sems.shape[0] - 3
    size = sens.shape[1] // pieces
    small = [
        pltpu.make_async_copy(source, target, sems.at[pieces + at])
        for at, (source, target) in enumerate(
            [(model_hbm, model), (observed_hbm, observed), (weight_hbm, weight)]
        )
    ]
    large = []
    for piece in range(pieces):
        lanes = pl.ds(piece * size, size)
        large.append(pltpu.make_async_copy(sens_hbm.at[:, lanes], sens.at[:, lanes], sems.at[piece]))
    small[0].start()
    for copy in large:
        copy.start()
    for copy in small[1:]:
        copy.start()
    small[0].wait()
    acc = predict_start(halves)
    for piece in range(pieces):
        large[piece].wait()
        chunks = size // LANES
        acc = predict(sens, model, halves, piece * chunks, chunks, acc)
    predict_store(acc, halves, out)
    for copy in small[1:]:
        copy.wait()
    wide = as_column(weight[...])
    station[0] = wide
    station[1] = as_column(observed[...])
    station[2] = scale[0] * wide


def first_terms_kernel(root_cells, parts, sens, station, out):
    halves = sens.shape[0] // SUB
    rows = out.shape[1] // 2
    weight, wide = weighted_residual(parts, station, root_cells)
    square = weight * weight

    def body(owner, carry):
        for row in range(rows):
            column = gradient = None
            for half in range(halves):
                block = chunk(sens, half, owner * rows + row)
                at = slice(half * SUB, (half + 1) * SUB)
                c = block * block * square[at]
                g = block * wide[at]
                column = c if column is None else column + c
                gradient = g if gradient is None else gradient + g
            out[owner, row : row + 1, :] = jnp.sum(column, axis=0, keepdims=True)
            out[owner, rows + row : rows + row + 1, :] = jnp.sum(gradient, axis=0, keepdims=True)
        return carry

    lax.fori_loop(0, out.shape[0], body, 0, unroll=2)


def second_terms_kernel(root_cells, parts, sens, station, out):
    halves = sens.shape[0] // SUB
    rows = out.shape[1]
    _, wide = weighted_residual(parts, station, root_cells)

    def body(owner, carry):
        for row in range(rows):
            gradient = None
            for half in range(halves):
                g = chunk(sens, half, owner * rows + row) * wide[half * SUB : (half + 1) * SUB]
                gradient = g if gradient is None else gradient + g
            out[owner, row : row + 1, :] = jnp.sum(gradient, axis=0, keepdims=True)
        return carry

    lax.fori_loop(0, out.shape[0], body, 0, unroll=4)


def sum_leading(ref):
    return jnp.sum(ref[...], axis=0)


def owner_sum_kernel(received, out):
    total = sum_leading(received)
    for peer in range(out.shape[0]):
        out[peer] = total


def message_kernel(rows, cell_blocks, owners, both, out):
    phys_count = both.shape[0] // cell_blocks
    size = out.shape[0] // owners
    cell_at = lax.axis_index("cell")
    part = LANES // phys_count
    lane = lax.broadcasted_iota(jnp.int32, (1, LANES), 1)
    gradient = maxima = None
    pieces = []
    for method in range(phys_count):
        block = both[method * cell_blocks + cell_at]
        pieces.append(block[:rows])
        gradient = block[rows:] if gradient is None else gradient + block[rows:]
        most = both[method * cell_blocks, :rows]
        for other in range(1, cell_blocks):
            most = jnp.maximum(most, both[method * cell_blocks + other, :rows])
        largest = jnp.max(jnp.max(most, axis=0, keepdims=True), axis=1, keepdims=True)
        largest = jnp.broadcast_to(largest, (1, LANES))
        maxima = largest if maxima is None else jnp.where(lane >= method * part, largest, maxima)
    message = jnp.concatenate(pieces + [gradient, maxima], axis=0)
    for row in range(size):
        wide = jnp.broadcast_to(message[row : row + 1], (owners, LANES))
        out[pl.ds(row, owners, stride=size), :] = wide


def model_kernel(rows, owners, phys_count, physics, root_stations, message, start, sens, parts, own, model, weights):
    position = lax.axis_index("sta")
    size = message.shape[0] // owners
    part = LANES // phys_count
    lane = lax.broadcasted_iota(jnp.int32, (1, LANES), 1)
    most = jnp.max(message[pl.ds(size - 1, owners, stride=size), :], axis=0, keepdims=True)
    scales = []
    for method in range(phys_count):
        inside = (lane >= method * part) & (lane < (method + 1) * part)
        largest = jnp.max(jnp.where(inside, most, 0.0), axis=1, keepdims=True)
        scales.append(1.0 / (largest + epsilon))
    for row in range(rows):
        relative = None
        for method in range(phys_count):
            column = message[pl.ds(method * rows + row, owners, stride=size), :]
            r = jnp.sqrt(column * scales[method])
            relative = r if relative is None else relative + r
        weight = weight_floor + relative / physics
        summed = message[pl.ds(phys_count * rows + row, owners, stride=size), :]
        at = pl.ds(row, owners, stride=rows)
        model[at, :] = start[at, :] - step_size * (summed / (root_stations * weight))
        weights[at, :] = weight
    halves = sens.shape[0] // SUB
    acc = predict(sens, model, halves, 0, model.shape[0], predict_start(halves))
    predict_store(acc, halves, parts)
    own_rows = pl.ds(position * rows, rows)
    own[0] = weights[own_rows, :]
    own[1] = model[own_rows, :]


def second_sum_kernel(received, out):
    out[...] = sum_leading(received)


def final_kernel(root_stations, summed, own, weight_out, gradient_out, model_out):
    total = sum_leading(summed)
    weight = own[0]
    gradient = total / (root_stations * weight)
    model = own[1] - step_size * gradient
    for row in range(total.shape[0]):
        lanes = slice(row * LANES, (row + 1) * LANES)
        weight_out[:, lanes] = weight[row : row + 1]
        gradient_out[:, lanes] = gradient[row : row + 1]
        model_out[:, lanes] = model[row : row + 1]


def kernel_call(kernel, name, outs, operands, scratch=(), spaces=None, kept=True):
    spaces = spaces or [pltpu.VMEM] * len(operands)
    operands = [
        pltpu.with_memory_space_constraint(x, space) if space == pltpu.HBM else x for x, space in zip(operands, spaces)
    ]
    make = pltpu.VMEM if kept else jax.ShapeDtypeStruct
    return pl.pallas_call(
        kernel,
        name=name,
        out_shape=[make(shape, jnp.float32) for shape in outs],
        in_specs=[pl.BlockSpec(memory_space=space) for space in spaces],
        out_specs=[pl.BlockSpec(memory_space=pltpu.VMEM)] * len(outs),
        scratch_shapes=scratch,
        compiler_params=pltpu.CompilerParams(vmem_limit_bytes=16 * 2**20),
    )(*operands)


def per_device(sensitivity, observed, data_weight, phys_weight, start_model):
    sta_count = lax.axis_size("sta")
    cell_blocks = lax.axis_size("cell")
    phys_count = lax.axis_size("phys")
    stations, cell_count = sensitivity.shape[1:]
    chunks = cell_count // LANES
    rows = chunks // sta_count
    physics = sensitivity.shape[0] * phys_count
    root_cells = math.sqrt(cell_count * cell_blocks)
    root_stations = math.sqrt(stations * sta_count)
    sens = sensitivity.reshape(stations, cell_count)
    start = start_model.reshape(chunks, LANES)
    size = rows * (phys_count + 1) + 1
    peers = phys_count * cell_blocks
    pieces = 8

    def swap(array, axes):
        return lax.all_to_all(array, axes, 0, 0, tiled=True)

    parts_shape = (cell_blocks, stations, LANES)
    parts, sens, station = kernel_call(
        predict_kernel,
        "predict",
        [parts_shape, (stations, cell_count), (3, stations, LANES)],
        [sens, start, observed, data_weight, phys_weight],
        scratch=[
            pltpu.VMEM((chunks, LANES), jnp.float32),
            pltpu.VMEM((1, stations), jnp.float32),
            pltpu.VMEM((1, stations), jnp.float32),
            pltpu.SemaphoreType.DMA((pieces + 3,)),
        ],
        spaces=[pltpu.HBM] * 4 + [pltpu.SMEM],
    )
    parts = swap(parts, "cell")
    (terms,) = kernel_call(
        functools.partial(first_terms_kernel, root_cells),
        "first_terms",
        [(sta_count, 2 * rows, LANES)],
        [parts, sens, station],
    )
    terms = swap(terms, "sta")
    (both,) = kernel_call(owner_sum_kernel, "owner_sum", [(peers, 2 * rows, LANES)], [terms])
    both = swap(both, ("phys", "cell"))
    (message,) = kernel_call(
        functools.partial(message_kernel, rows, cell_blocks, sta_count),
        "message",
        [(sta_count * size, LANES)],
        [both],
    )
    message = swap(message.reshape(sta_count, 1, size * LANES), "sta").reshape(sta_count * size, LANES)
    parts, own = kernel_call(
        functools.partial(model_kernel, rows, sta_count, phys_count, physics, root_stations),
        "model",
        [parts_shape, (2, rows, LANES)],
        [message, start, sens],
        scratch=[pltpu.VMEM((chunks, LANES), jnp.float32)] * 2,
    )
    parts = swap(parts, "cell")
    (terms,) = kernel_call(
        functools.partial(second_terms_kernel, root_cells),
        "second_terms",
        [(sta_count, rows, LANES)],
        [parts, sens, station],
    )
    terms = swap(terms, "sta")
    (summed,) = kernel_call(second_sum_kernel, "second_sum", [(rows, LANES)], [terms])
    summed = lax.all_gather(summed, "phys")
    out = (1, rows * LANES)
    return tuple(
        kernel_call(functools.partial(final_kernel, root_stations), "final", [out] * 3, [summed, own], kept=False)
    )


def solution(mesh):
    return jax.shard_map(
        per_device,
        mesh=mesh,
        in_specs=(
            P("phys", "sta", "cell"),
            P("phys", "sta"),
            P("phys", "sta"),
            P("phys"),
            P("cell"),
        ),
        out_specs=(P("cell", "sta"), P("cell", "sta"), P("cell", "sta")),
        check_vma=False,
    )
```

time: 108 us -> 104 us (0.963)
  blocking collectives: 90.7 us -> 97.6 us
  starting transfers between devices: 4.84 us -> 0 us
  waiting for transfers between devices: 3.65 us -> 0 us
  local copies, waits for them, and re-layouts: 2.52 us -> 0.01 us
    all_to_all x5 -> x6, blocking collectives: 85.5 us -> 92.3 us  [swap(): return lax.all_to_all(array, axes, 0, 0, tiled=True)]
    all_to_all x1 -> x0, starting transfers between devices: 4.84 us -> none  [swap(): return lax.all_to_all(array, axes, 0, 0, tiled=True)]
    all_to_all x1 -> x0, waiting for transfers between devices: 3.65 us -> none  [swap(): return lax.all_to_all(array, axes, 0, 0, tiled=True)]
    unnamed x12 -> x2, local copies, waits for them, and re-layouts: 2.52 us -> 0.01 us
  transfers between devices with their start and end apart: 1 -> 0, of which waited for: 1 -> 0; matrix products, arithmetic and copies ran while one was open for 0% -> 0% of each run, Pallas kernels for 0% -> 0%
where the time goes in v3:
time: 104 us
  blocking collectives  97.6 us (94%)
  Pallas kernels  4.79 us (5%)
  between operations  1.32 us (1%)
    all_to_all x6, blocking collectives, swap(): return lax.all_to_all(array, axes, 0, 0, tiled=True)  92.3 us
    all_gather x1, blocking collectives, per_device(): summed = lax.all_gather(summed, 'phys')  5.31 us
    pallas_call x8, Pallas kernels, kernel_call(): pl.pallas_call(kernel, name=name, out_shape=[make(shape, jnp.float32) for...  4.79 us

profile of v3, /device:TPU:1, one launch (start us, length us, event | category | flops | bytes accessed | tf_op | source)
XLA Modules:
  0.0 103.7 jit_solution(12286628745732450498)
XLA Ops:
  1.3 1.8 %predict.1 = (f32[4,16,128]{2,1,0:T(8,128)S(1)}, f32[16,32768]{1,0:T(8,128)S(1)}, f32[3,16,128]{2,1,0:T(8,128)S(1)}) custom-call(f32[16,32768]{1,0:T(8,128)} %bitcast.10, f32[256,128]{1,0:T(8,128)} %bitcast.7, f32[1,16]{1,0:T(1,128)} %observed_hbm.1, f32[1,16]{1,0:T(1,128)} %weight_hbm.1, f32[1]{0:T(128)S(6)} %copy.9.scale), custom_call_target="tpu_custom_call" | custom-call | tf_op jit(solution)/shard_map/predict/pallas_call | solution.py:228
  3.1 8.9 %all_to_all.30.parts = f32[4,16,128]{2,1,0:T(8,128)S(1)} all-to-all(f32[4,16,128]{2,1,0:T(8,128)S(1)} %get-tuple-element.8), channel_id=1, replica_groups=mesh['phys'=2,'sta'=64,'cell'=4] {'cell'}, dimensions={0} | all-to-all | bytes 65536 | tf_op jit(solution)/shard_map/all_to_all | solution.py:256
  12.0 0.0 copy-start
  12.0 1.0 first_terms.1
  13.1 28.6 %all_to_all.31.received = f32[64,8,128]{2,1,0:T(8,128)S(1)} all-to-all(f32[64,8,128]{2,1,0:T(8,128)S(1)} %first_terms.1), channel_id=1, replica_groups=mesh['phys'=2,'sta'=64,'cell'=4] {'sta'}, dimensions={0} | all-to-all | bytes 524288 | tf_op jit(solution)/shard_map/all_to_all | solution.py:256
  41.7 0.1 owner_sum.1
  41.7 10.8 %all_to_all.32.both = f32[8,8,128]{2,1,0:T(8,128)S(1)} all-to-all(f32[8,8,128]{2,1,0:T(8,128)S(1)} %owner_sum.1), channel_id=1, replica_groups=mesh['phys'=2,'sta'=64,'cell'=4] {'phys','cell'}, dimensions={0} | all-to-all | bytes 65536 | tf_op jit(solution)/shard_map/all_to_all | solution.py:256
  52.6 0.1 message.1
  52.7 20.0 %all_to_all.33 = f32[64,1,1664]{2,1,0:T(1,128)S(1)} all-to-all(f32[64,1,1664]{2,1,0:T(1,128)S(1)} %bitcast.5), channel_id=1, replica_groups=mesh['phys'=2,'sta'=64,'cell'=4] {'sta'}, dimensions={0} | all-to-all | bytes 851968 | tf_op jit(solution)/shard_map/all_to_all | solution.py:256
  72.7 0.0 copy-done
  72.7 0.6 model.1
  73.3 6.7 %all_to_all.34.parts = f32[4,16,128]{2,1,0:T(8,128)S(1)} all-to-all(f32[4,16,128]{2,1,0:T(8,128)S(1)} %get-tuple-element.11), channel_id=1, replica_groups=mesh['phys'=2,'sta'=64,'cell'=4] {'cell'}, dimensions={0} | all-to-all | bytes 65536 | tf_op jit(solution)/shard_map/all_to_all | solution.py:256
  80.0 0.5 second_terms.1
  80.5 17.2 %all_to_all.35.received = f32[64,4,128]{2,1,0:T(4,128)S(1)} all-to-all(f32[64,4,128]{2,1,0:T(4,128)S(1)} %second_terms.1), channel_id=1, replica_groups=mesh['phys'=2,'sta'=64,'cell'=4] {'sta'}, dimensions={0} | all-to-all | bytes 262144 | tf_op jit(solution)/shard_map/all_to_all | solution.py:256
  97.7 0.1 second_sum.1
  97.8 5.3 %all-gather.1.summed = f32[2,4,128]{2,1,0:T(4,128)S(1)} all-gather(f32[1,4,128]{2,1,0:T(4,128)S(1)} %bitcast.9), channel_id=2, replica_groups=mesh['phys'=2,'sta'=64,'cell'=4] {'phys'}, dimensions={0}, use_global_device_ids=true | all-gather | bytes 6144 | tf_op jit(solution)/shard_map/all_gather | solution.py:305
  103.1 0.6 final.1
Async XLA Ops:
  12.0 60.7 %copy-start = (f32[32768]{0:T(1024)S(1)}, f32[32768]{0:T(1024)}, u32[]{:S(2)}) copy-start(f32[32768]{0:T(1024)} %param.9) | copy-start | bytes 393220

commit v4 on v0

v4 whole, which is shorter than its diff:
```python
import functools
import math

import jax
import jax.numpy as jnp
from jax import lax
from jax.experimental import pallas as pl
from jax.experimental.pallas import tpu as pltpu
from jax.sharding import PartitionSpec as P

ITERS = 2
LANES = 128
SUB = 8

step_size = 0.5
weight_floor = 0.1
epsilon = 1e-06


def lane_index(rows):
    return lax.broadcasted_iota(jnp.int32, (rows, LANES), 1)


def as_column(row):
    stations = row.shape[1]
    wide = jnp.broadcast_to(row, (stations, stations))
    at = lax.broadcasted_iota(jnp.int32, (stations, stations), 0)
    to = lax.broadcasted_iota(jnp.int32, (stations, stations), 1)
    return jnp.sum(jnp.where(at == to, wide, 0.0), axis=1, keepdims=True)


def in_lanes(columns):
    lane = lane_index(columns[0].shape[0])
    tile = jnp.zeros(lane.shape, jnp.float32)
    for at, column in enumerate(columns):
        tile = jnp.where(lane == at, column, tile)
    return tile


def lanes_of(chunk):
    return pl.ds(chunk * LANES, LANES)


def store_row(out, at, value):
    out[pl.ds(at, 1), :] = jnp.sum(value, axis=0, keepdims=True)


def predict_kernel(
    rows, sens_hbm, model_hbm, observed_hbm, weight_hbm, scale, out, sens, send, model, observed, weight, sems
):
    halves, pieces = sens.shape[0] // SUB, sems.shape[0] - 3
    size = sens.shape[1] // pieces
    share = rows // 2
    core = lax.axis_index("phys")
    small = [
        pltpu.make_async_copy(source, target, sems.at[pieces + at])
        for at, (source, target) in enumerate(
            [(model_hbm, model), (observed_hbm, observed), (weight_hbm, weight)]
        )
    ]
    large = []
    for piece in range(pieces):
        lanes = pl.ds(piece * size, size)
        large.append(pltpu.make_async_copy(sens_hbm.at[:, lanes], sens.at[:, lanes], sems.at[piece]))
    small[0].start()
    for copy in large:
        copy.start()
    for copy in small[1:]:
        copy.start()
    small[0].wait()
    owners = size // LANES // rows

    def body(owner, acc):
        acc = list(acc)
        for row in range(rows):
            at = owner * rows + row
            value = model[pl.ds(at, 1), :]
            for half in range(halves):
                slot = (row % 4) * halves + half
                acc[slot] = acc[slot] + sens[half * SUB : (half + 1) * SUB, lanes_of(at)] * value
        for row in range(share):
            source = lanes_of(owner * rows + (1 - core) * share + row)
            send[:, lanes_of(owner * share + row)] = sens[:, source]
        return tuple(acc)

    acc = (jnp.zeros((SUB, LANES), jnp.float32),) * (4 * halves)
    for piece in range(pieces):
        large[piece].wait()
        acc = lax.fori_loop(piece * owners, (piece + 1) * owners, body, acc, unroll=4)
    total = [
        (acc[half] + acc[halves + half]) + (acc[2 * halves + half] + acc[3 * halves + half]) for half in range(halves)
    ]
    part = jnp.sum(jnp.concatenate(total, axis=0), axis=1, keepdims=True)
    for copy in small[1:]:
        copy.wait()
    column = as_column(weight[...])
    tile = in_lanes([part, column, as_column(observed[...]), scale[0] * column])
    for peer in range(out.shape[0]):
        out[peer] = tile


def residual_weights(predicted, station):
    weight, observed, scaled = station[:, 1:2], station[:, 2:3], station[:, 3:4]
    residual = weight * (predicted - observed)
    shape = (station.shape[0], LANES)
    return jnp.broadcast_to(weight, shape), jnp.broadcast_to(scaled * residual, shape)


def first_terms_kernel(rows, owners, cell_blocks, root_cells, parts, sens, got, out):
    halves = sens.shape[0] // SUB
    share = rows // 2
    core = lax.axis_index("phys")
    squares, wides = [], []
    for method in (core, 1 - core):
        station = parts[method * cell_blocks]
        total = station
        for block in range(1, cell_blocks):
            total = total + parts[method * cell_blocks + block]
        weight, wide = residual_weights(total[:, 0:1] / root_cells, station)
        squares.append(weight * weight)
        wides.append(wide)

    def body(owner, carry):
        for row in range(share):
            sources = (
                (sens, lanes_of(owner * rows + core * share + row)),
                (got, lanes_of(owner * share + row)),
            )
            gradient = None
            for method, (source, lanes) in enumerate(sources):
                column = None
                for half in range(halves):
                    at = slice(half * SUB, (half + 1) * SUB)
                    block = source[at, lanes]
                    c = block * block * squares[method][at]
                    g = block * wides[method][at]
                    column = c if column is None else column + c
                    gradient = g if gradient is None else gradient + g
                store_row(out, (owner * 3 + method) * share + row, column)
            store_row(out, (owner * 3 + 2) * share + row, gradient)
        return carry

    lax.fori_loop(0, owners, body, 0, unroll=4)


def owner_sum_kernel(rows, owners, received, own, out):
    share = rows // 2
    core = lax.axis_index("phys")
    size = 3 * share
    for row in range(size):
        own[row : row + 1, :] = jnp.sum(received[pl.ds(row, owners, stride=size), :], axis=0, keepdims=True)
    largest = []
    for method in range(2):
        most = jnp.max(own[method * share : (method + 1) * share, :], axis=0, keepdims=True)
        largest.append(jnp.max(most, axis=1, keepdims=True))
    first = jnp.where(core == 0, largest[0], largest[1])
    second = jnp.where(core == 0, largest[1], largest[0])
    tile = jnp.where(lane_index(1) < LANES // 2, first, second)
    for peer in range(out.shape[0]):
        out[peer] = tile


def message_kernel(owners, maxima, own, out):
    size = own.shape[0] + 1
    most = maxima[0]
    for peer in range(1, maxima.shape[0]):
        most = jnp.maximum(most, maxima[peer])
    for row in range(size):
        value = own[row : row + 1, :] if row < size - 1 else most
        out[pl.ds(row, owners, stride=size), :] = jnp.broadcast_to(value, (owners, LANES))


def model_kernel(rows, owners, physics, root_stations, message, start, sens, got, out, own, model, weights):
    halves = sens.shape[0] // SUB
    share = rows // 2
    core = lax.axis_index("phys")
    position = lax.axis_index("sta")
    size = message.shape[0] // owners
    most = jnp.max(message[pl.ds(size - 1, owners, stride=size), :], axis=0, keepdims=True)
    first_lanes = lane_index(1) < LANES // 2
    scales = []
    for method in (core, 1 - core):
        inside = first_lanes == (method == 0)
        largest = jnp.max(jnp.where(inside, most, 0.0), axis=1, keepdims=True)
        scales.append(1.0 / (largest + epsilon))
    for row in range(share):
        relative = None
        for method in range(2):
            column = message[pl.ds(method * share + row, owners, stride=size), :]
            r = jnp.sqrt(column * scales[method])
            relative = r if relative is None else relative + r
        weight = weight_floor + relative / physics
        summed = message[pl.ds(2 * share + row, owners, stride=size), :]
        before = [start[pl.ds(at * share + row, owners, stride=rows), :] for at in range(2)]
        at = pl.ds(row, owners, stride=share)
        model[at, :] = jnp.where(core == 0, before[0], before[1]) - step_size * (summed / (root_stations * weight))
        weights[at, :] = weight

    def body(owner, acc):
        acc = list(acc)
        for row in range(share):
            value = model[pl.ds(owner * share + row, 1), :]
            sources = (
                (sens, lanes_of(owner * rows + core * share + row)),
                (got, lanes_of(owner * share + row)),
            )
            for method, (source, lanes) in enumerate(sources):
                for half in range(halves):
                    slot = ((row % 2) * 2 + method) * halves + half
                    acc[slot] = acc[slot] + source[half * SUB : (half + 1) * SUB, lanes] * value
        return tuple(acc)

    acc = (jnp.zeros((SUB, LANES), jnp.float32),) * (4 * halves)
    acc = lax.fori_loop(0, owners, body, acc, unroll=4)
    columns = []
    for method in range(2):
        total = [acc[method * halves + half] + acc[(2 + method) * halves + half] for half in range(halves)]
        columns.append(jnp.sum(jnp.concatenate(total, axis=0), axis=1, keepdims=True))
    lane = lane_index(columns[0].shape[0])
    tile = jnp.where(lane == core, columns[0], jnp.where(lane == 1 - core, columns[1], 0.0))
    for peer in range(out.shape[0]):
        out[peer] = tile
    own_rows = pl.ds(position * share, share)
    own[0] = weights[own_rows, :]
    own[1] = model[own_rows, :]


def second_terms_kernel(rows, owners, cell_blocks, root_cells, parts, stations, sens, got, out):
    halves = sens.shape[0] // SUB
    share = rows // 2
    core = lax.axis_index("phys")
    total = parts[0]
    for peer in range(1, parts.shape[0]):
        total = total + parts[peer]
    lane = lane_index(total.shape[0])
    wides = []
    for method in (core, 1 - core):
        predicted = jnp.sum(jnp.where(lane == method, total, 0.0), axis=1, keepdims=True) / root_cells
        wides.append(residual_weights(predicted, stations[method * cell_blocks])[1])

    def body(owner, carry):
        for row in range(share):
            sources = (
                (sens, lanes_of(owner * rows + core * share + row)),
                (got, lanes_of(owner * share + row)),
            )
            gradient = None
            for method, (source, lanes) in enumerate(sources):
                for half in range(halves):
                    at = slice(half * SUB, (half + 1) * SUB)
                    g = source[at, lanes] * wides[method][at]
                    gradient = g if gradient is None else gradient + g
            store_row(out, owner * share + row, gradient)
        return carry

    lax.fori_loop(0, owners, body, 0, unroll=4)


def second_step_kernel(owners, root_stations, received, own, out):
    share = own.shape[1]
    for row in range(share):
        total = jnp.sum(received[pl.ds(row, owners, stride=share), :], axis=0, keepdims=True)
        weight = own[0, row : row + 1, :]
        gradient = total / (root_stations * weight)
        out[row : row + 1, :] = weight
        out[share + row : share + row + 1, :] = gradient
        out[2 * share + row : 2 * share + row + 1, :] = own[1, row : row + 1, :] - step_size * gradient


def layout_kernel(both, *outs):
    share = both.shape[1] // len(outs)
    for at, out in enumerate(outs):
        for core in range(both.shape[0]):
            for row in range(share):
                to = (core * share + row) * LANES
                source = at * share + row
                out[:, to : to + LANES] = both[core, source : source + 1, :]


def kernel_call(kernel, name, outs, operands, scratch=(), spaces=None, kept=True):
    make = pltpu.VMEM if kept else jax.ShapeDtypeStruct
    spaces = spaces or [pltpu.VMEM] * len(operands)
    operands = [
        pltpu.with_memory_space_constraint(x, space) if space == pltpu.HBM else x for x, space in zip(operands, spaces)
    ]
    return pl.pallas_call(
        kernel,
        name=name,
        out_shape=[make(shape, jnp.float32) for shape in outs],
        in_specs=[pl.BlockSpec(memory_space=space) for space in spaces],
        out_specs=[pl.BlockSpec(memory_space=pltpu.VMEM)] * len(outs),
        scratch_shapes=scratch,
        compiler_params=pltpu.CompilerParams(vmem_limit_bytes=16 * 2**20),
    )(*operands)


def per_device(sensitivity, observed, data_weight, phys_weight, start_model):
    owners = lax.axis_size("sta")
    cell_blocks = lax.axis_size("cell")
    physics = sensitivity.shape[0] * lax.axis_size("phys")
    stations, cell_count = sensitivity.shape[1:]
    chunks = cell_count // LANES
    rows = chunks // owners
    share = rows // 2
    root_cells = math.sqrt(cell_count * cell_blocks)
    root_stations = math.sqrt(stations * owners)
    sens = sensitivity.reshape(stations, cell_count)
    start = start_model.reshape(chunks, LANES)
    peers = physics * cell_blocks
    pieces = min(8, owners)

    def swap(array, axes):
        return lax.all_to_all(array, axes, 0, 0, tiled=True)

    def swap_rows(array):
        return swap(array.reshape(owners, 1, -1), "sta").reshape(array.shape)

    parts_shape = (peers, stations, LANES)
    first, sens, send = kernel_call(
        functools.partial(predict_kernel, rows),
        "predict",
        [parts_shape, (stations, cell_count), (stations, cell_count // 2)],
        [sens, start, observed, data_weight, phys_weight],
        scratch=[
            pltpu.VMEM((chunks, LANES), jnp.float32),
            pltpu.VMEM((1, stations), jnp.float32),
            pltpu.VMEM((1, stations), jnp.float32),
            pltpu.SemaphoreType.DMA((pieces + 3,)),
        ],
        spaces=[pltpu.HBM] * 4 + [pltpu.SMEM],
    )
    got = lax.ppermute(send, "phys", [(0, 1), (1, 0)])
    first = swap(first, ("phys", "cell"))
    (terms,) = kernel_call(
        functools.partial(first_terms_kernel, rows, owners, cell_blocks, root_cells),
        "first_terms",
        [(owners * 3 * share, LANES)],
        [first, sens, got],
    )
    own, maxima = kernel_call(
        functools.partial(owner_sum_kernel, rows, owners),
        "owner_sum",
        [(3 * share, LANES), (peers, 1, LANES)],
        [swap_rows(terms)],
    )
    (message,) = kernel_call(
        functools.partial(message_kernel, owners),
        "message",
        [(owners * (3 * share + 1), LANES)],
        [swap(maxima, ("phys", "cell")), own],
    )
    second, own = kernel_call(
        functools.partial(model_kernel, rows, owners, physics, root_stations),
        "model",
        [parts_shape, (2, share, LANES)],
        [swap_rows(message), start, sens, got],
        scratch=[pltpu.VMEM((chunks // 2, LANES), jnp.float32)] * 2,
    )
    (terms,) = kernel_call(
        functools.partial(second_terms_kernel, rows, owners, cell_blocks, root_cells),
        "second_terms",
        [(owners * share, LANES)],
        [swap(second, ("phys", "cell")), first, sens, got],
    )
    (halves,) = kernel_call(
        functools.partial(second_step_kernel, owners, root_stations),
        "second_step",
        [(3 * share, LANES)],
        [swap_rows(terms), own],
    )
    return tuple(
        kernel_call(layout_kernel, "layout", [(1, rows * LANES)] * 3, [lax.all_gather(halves, "phys")], kept=False)
    )


def solution(mesh):
    return jax.shard_map(
        per_device,
        mesh=mesh,
        in_specs=(
            P("phys", "sta", "cell"),
            P("phys", "sta"),
            P("phys", "sta"),
            P("phys"),
            P("cell"),
        ),
        out_specs=(P("cell", "sta"), P("cell", "sta"), P("cell", "sta")),
        check_vma=False,
    )
```

time: 436 us -> 103 us (0.24)
  waiting for transfers between devices: 376 us -> 0.01 us
  blocking collectives: 25.7 us -> 85.8 us
  between operations: 15.2 us -> 1.32 us
  matrix products: 12.1 us -> 0 us
  starting transfers between devices: 0.16 us -> 8.79 us
  Pallas kernels: 0 us -> 6.72 us
  other arithmetic: 6.22 us -> 0 us
    psum x4 -> x0, waiting for transfers between devices: 376 us -> none  [the longest x2 186 us: per_device(): summed = lax.psum(lax.psum(partial_value, 'sta'), 'phys')]
    all_to_all x0 -> x6, blocking collectives: none -> 82.8 us  [swap(): return lax.all_to_all(array, axes, 0, 0, tiled=True)]
    psum x2 -> x0, blocking collectives: 16.7 us -> none  [per_device(): predicted = lax.psum(local_pred, 'cell') / root_cells]
    dot_general x5 -> x0, matrix products: 12.1 us -> none  [the longest x2 6.66 us: per_device(): jnp.einsum('psc,c->ps', sensitivity, model_full, precision=highest)]
    pmax x1 -> x0, blocking collectives: 9.01 us -> none  [per_device(): column_max = lax.pmax(jnp.max(column_full, axis=1), 'cell')]
    ppermute x0 -> x1, starting transfers between devices: none -> 8.79 us  [per_device(): got = lax.ppermute(send, 'phys', [(0, 1), (1, 0)])]
    pallas_call x0 -> x8, Pallas kernels: none -> 6.72 us  [kernel_call(): pl.pallas_call(kernel, name=name, out_shape=[make(shape, jnp.float32) for...]
  transfers between devices with their start and end apart: 4 -> 1, of which waited for: 4 -> 0; matrix products, arithmetic and copies ran while one was open for 0% -> 0% of each run, Pallas kernels for 0% -> 0%
where the time goes in v4:
time: 103 us
  blocking collectives  85.8 us (83%)
  starting transfers between devices  8.79 us (9%)
  Pallas kernels  6.72 us (7%)
  between operations  1.32 us (1%)
    all_to_all x6, blocking collectives, swap(): return lax.all_to_all(array, axes, 0, 0, tiled=True)  82.8 us
    ppermute x1, starting transfers between devices, per_device(): got = lax.ppermute(send, 'phys', [(0, 1), (1, 0)])  8.79 us
    pallas_call x8, Pallas kernels, kernel_call(): pl.pallas_call(kernel, name=name, out_shape=[make(shape, jnp.float32) for...  6.72 us
    all_gather x1, blocking collectives, per_device(): lax.all_gather(halves, 'phys')  3.03 us
  transfers between devices with their start and end apart: 1, of which 0 were waited for; matrix products, arithmetic and copies ran while one was open for 0% of the time, Pallas kernels for 0%

profile of v4, /device:TPU:1, one launch (start us, length us, event | category | flops | bytes accessed | tf_op | source)
XLA Modules:
  0.0 102.7 jit_solution(7931661999830714588)
XLA Ops:
  1.3 1.9 %predict.1 = (f32[8,16,128]{2,1,0:T(8,128)S(1)}, f32[16,32768]{1,0:T(8,128)S(1)}, f32[16,16384]{1,0:T(8,128)S(1)}) custom-call(f32[16,32768]{1,0:T(8,128)} %bitcast.18, f32[256,128]{1,0:T(8,128)} %bitcast.13, f32[1,16]{1,0:T(1,128)} %observed_hbm.1, f32[1,16]{1,0:T(1,128)} %weight_hbm.1, f32[1]{0:T(128)S(6)} %copy.11.scale), custom_call_target="tpu_custom_call" | custom-call | tf_op jit(solution)/shard_map/predict/pallas_call | solution.py:286
  3.2 8.8 %collective-permute-start = (f32[16,16384]{1,0:T(8,128)S(1)}, f32[16,16384]{1,0:T(8,128)S(1)}, u32[]{:S(2)}, u32[]{:S(2)}) collective-permute-start(f32[16,16384]{1,0:T(8,128)S(1)} %get-tuple-element.12), channel_id=1, source_target_pairs={{0,256},{256,0},{1,257},{257,1},{2,258},{258,2},{3,259},{259,3},{4... | collective-permute-start | bytes 3145736 | tf_op jit(solution)/shard_map/ppermute | solution.py:332
  12.0 7.3 %all_to_all.30.parts.stations = f32[8,16,128]{2,1,0:T(8,128)S(1)} all-to-all(f32[8,16,128]{2,1,0:T(8,128)S(1)} %get-tuple-element.10), channel_id=1, replica_groups=mesh['phys'=2,'sta'=64,'cell'=4] {'phys','cell'}, dimensions={0} | all-to-all | bytes 131072 | tf_op jit(solution)/shard_map/all_to_all | solution.py:313
  19.4 0.0 collective-permute-done.got
  19.4 0.0 copy-start
  19.4 1.7 %first_terms.1 = f32[384,128]{1,0:T(8,128)S(1)} custom-call(f32[8,16,128]{2,1,0:T(8,128)S(1)} %all_to_all.30.parts.stations, f32[16,32768]{1,0:T(8,128)S(1)} %get-tuple-element.11.sens, f32[16,16384]{1,0:T(8,128)S(1)} %collective-permute-done.got), custom_call_target="tpu_custom_call" | custom-call | tf_op jit(solution)/shard_map/first_terms/pallas_call | solution.py:286
  21.1 24.7 %all_to_all.31 = f32[64,1,768]{2,1,0:T(1,128)S(1)} all-to-all(f32[64,1,768]{2,1,0:T(1,128)S(1)} %bitcast.12), channel_id=1, replica_groups=mesh['phys'=2,'sta'=64,'cell'=4] {'sta'}, dimensions={0} | all-to-all | bytes 393216 | tf_op jit(solution)/shard_map/all_to_all | solution.py:313
  45.8 0.1 owner_sum.1
  45.9 9.5 %all_to_all.32.maxima = f32[8,1,128]{2,1,0:T(1,128)S(1)} all-to-all(f32[8,1,128]{2,1,0:T(1,128)S(1)} %get-tuple-element.13), channel_id=1, replica_groups=mesh['phys'=2,'sta'=64,'cell'=4] {'phys','cell'}, dimensions={0} | all-to-all | bytes 8192 | tf_op jit(solution)/shard_map/all_to_all | solution.py:313
  55.4 16.4 %all_to_all.33 = f32[64,1,896]{2,1,0:T(1,128)S(1)} all-to-all(f32[64,1,896]{2,1,0:T(1,128)S(1)} %bitcast.9), channel_id=1, replica_groups=mesh['phys'=2,'sta'=64,'cell'=4] {'sta'}, dimensions={0} | all-to-all | bytes 458752 | tf_op jit(solution)/shard_map/all_to_all | solution.py:313
  71.7 0.0 copy-done
  71.7 0.6 model.1
  72.4 10.0 %all_to_all.34.parts = f32[8,16,128]{2,1,0:T(8,128)S(1)} all-to-all(f32[8,16,128]{2,1,0:T(8,128)S(1)} %get-tuple-element.15), channel_id=1, replica_groups=mesh['phys'=2,'sta'=64,'cell'=4] {'phys','cell'}, dimensions={0} | all-to-all | bytes 131072 | tf_op jit(solution)/shard_map/all_to_all | solution.py:313
  82.4 1.7 %second_terms.1 = f32[128,128]{1,0:T(8,128)S(1)} custom-call(f32[8,16,128]{2,1,0:T(8,128)S(1)} %all_to_all.34.parts, f32[8,16,128]{2,1,0:T(8,128)S(1)} %all_to_all.30.parts.stations, f32[16,32768]{1,0:T(8,128)S(1)} %get-tuple-element.11.sens, f32[16,16384]{1,0:T(8,128)S(1)} %collective-permute-done.got), custom_call_target="tpu_custom_call" | custom-call | tf_op jit(solution)/shard_map/second_terms/pallas_call | solution.py:286
  84.1 14.9 %all_to_all.35 = f32[64,1,256]{2,1,0:T(1,128)S(1)} all-to-all(f32[64,1,256]{2,1,0:T(1,128)S(1)} %bitcast.15), channel_id=1, replica_groups=mesh['phys'=2,'sta'=64,'cell'=4] {'sta'}, dimensions={0} | all-to-all | bytes 131072 | tf_op jit(solution)/shard_map/all_to_all | solution.py:313
  99.0 3.0 %all-gather.1.both = f32[2,6,128]{2,1,0:T(8,128)S(1)} all-gather(f32[1,6,128]{2,1,0:T(8,128)S(1)} %bitcast.17), channel_id=2, replica_groups=mesh['phys'=2,'sta'=64,'cell'=4] {'phys'}, dimensions={0}, use_global_device_ids=true | all-gather | bytes 9216 | tf_op jit(solution)/shard_map/all_gather | solution.py:372
  102.1 0.6 layout.1
  (2 shorter events, 0.0 us)
Async XLA Ops:
  3.2 16.1 %collective-permute-start = (f32[16,16384]{1,0:T(8,128)S(1)}, f32[16,16384]{1,0:T(8,128)S(1)}, u32[]{:S(2)}, u32[]{:S(2)}) collective-permute-start(f32[16,16384]{1,0:T(8,128)S(1)} %get-tuple-element.12), channel_id=1, source_target_pairs={{0,256},{256,0},{1,257},{257,1},{2,258},{258,2},{3,259},{259,3},{4... | collective-permute-start | bytes 3145736 | tf_op jit(solution)/shard_map/ppermute | solution.py:332
  19.4 52.4 %copy-start = (f32[32768]{0:T(1024)S(1)}, f32[32768]{0:T(1024)}, u32[]{:S(2)}) copy-start(f32[32768]{0:T(1024)} %param.9) | copy-start | bytes 393220

commit v5 on v4

--- a/solution.py
+++ b/solution.py
@@ -41,8 +41,26 @@
     return pl.ds(chunk * LANES, LANES)
 
 
-def store_row(out, at, value):
-    out[pl.ds(at, 1), :] = jnp.sum(value, axis=0, keepdims=True)
+def fold(values):
+    row = lax.broadcasted_iota(jnp.int32, (SUB, LANES), 0)
+    skewed = [values[-at % SUB] for at in range(SUB)]
+    for shift in (1, 2, 4):
+        moves = (row & shift) != 0
+        skewed = [jnp.where(moves, skewed[(at - shift) % SUB], skewed[at]) for at in range(SUB)]
+    terms = [skewed[0]] + [pltpu.roll(skewed[at], SUB - at, 0) for at in range(1, SUB)]
+    return ((terms[0] + terms[1]) + (terms[2] + terms[3])) + ((terms[4] + terms[5]) + (terms[6] + terms[7]))
+
+
+def store_tiles(owners, size, owner_rows, out):
+    group = SUB // math.gcd(SUB, size)
+    tiles = group * size // SUB
+
+    for step in range(owners // group):
+        values = []
+        for member in range(group):
+            values += owner_rows(step * group + member)
+        for tile in range(tiles):
+            out[step * tiles + tile] = fold(values[tile * SUB : (tile + 1) * SUB])
 
 
 def predict_kernel(
@@ -86,7 +104,8 @@
     acc = (jnp.zeros((SUB, LANES), jnp.float32),) * (4 * halves)
     for piece in range(pieces):
         large[piece].wait()
-        acc = lax.fori_loop(piece * owners, (piece + 1) * owners, body, acc, unroll=4)
+        for owner in range(piece * owners, (piece + 1) * owners):
+            acc = body(owner, acc)
     total = [
         (acc[half] + acc[halves + half]) + (acc[2 * halves + half] + acc[3 * halves + half]) for half in range(halves)
     ]
@@ -103,24 +122,22 @@
     weight, observed, scaled = station[:, 1:2], station[:, 2:3], station[:, 3:4]
     residual = weight * (predicted - observed)
     shape = (station.shape[0], LANES)
-    return jnp.broadcast_to(weight, shape), jnp.broadcast_to(scaled * residual, shape)
-
-
-def first_terms_kernel(rows, owners, cell_blocks, root_cells, parts, sens, got, out):
+    return jnp.broadcast_to(weight * weight, shape), jnp.broadcast_to(scaled * residual, shape)
+
+
+def first_terms_kernel(rows, owners, cell_blocks, root_cells, parts, sens, got, out, wide):
     halves = sens.shape[0] // SUB
     share = rows // 2
     core = lax.axis_index("phys")
-    squares, wides = [], []
-    for method in (core, 1 - core):
+    for place, method in enumerate((core, 1 - core)):
         station = parts[method * cell_blocks]
         total = station
         for block in range(1, cell_blocks):
             total = total + parts[method * cell_blocks + block]
-        weight, wide = residual_weights(total[:, 0:1] / root_cells, station)
-        squares.append(weight * weight)
-        wides.append(wide)
-
-    def body(owner, carry):
+        wide[place], wide[2 + place] = residual_weights(total[:, 0:1] / root_cells, station)
+
+    def owner_rows(owner):
+        columns, gradients = ([], []), []
         for row in range(share):
             sources = (
                 (sens, lanes_of(owner * rows + core * share + row)),
@@ -132,15 +149,15 @@
                 for half in range(halves):
                     at = slice(half * SUB, (half + 1) * SUB)
                     block = source[at, lanes]
-                    c = block * block * squares[method][at]
-                    g = block * wides[method][at]
+                    c = block * block * wide[method, at, :]
+                    g = block * wide[2 + method, at, :]
                     column = c if column is None else column + c
                     gradient = g if gradient is None else gradient + g
-                store_row(out, (owner * 3 + method) * share + row, column)
-            store_row(out, (owner * 3 + 2) * share + row, gradient)
-        return carry
-
-    lax.fori_loop(0, owners, body, 0, unroll=4)
+                columns[method].append(column)
+            gradients.append(gradient)
+        return columns[0] + columns[1] + gradients
+
+    store_tiles(owners, 3 * share, owner_rows, out)
 
 
 def owner_sum_kernel(rows, owners, received, own, out):
@@ -211,7 +228,8 @@
         return tuple(acc)
 
     acc = (jnp.zeros((SUB, LANES), jnp.float32),) * (4 * halves)
-    acc = lax.fori_loop(0, owners, body, acc, unroll=4)
+    for owner in range(owners):
+        acc = body(owner, acc)
     columns = []
     for method in range(2):
         total = [acc[method * halves + half] + acc[(2 + method) * halves + half] for half in range(halves)]
@@ -225,7 +243,7 @@
     own[1] = model[own_rows, :]
 
 
-def second_terms_kernel(rows, owners, cell_blocks, root_cells, parts, stations, sens, got, out):
+def second_terms_kernel(rows, owners, cell_blocks, root_cells, parts, stations, sens, got, out, wide):
     halves = sens.shape[0] // SUB
     share = rows // 2
     core = lax.axis_index("phys")
@@ -233,12 +251,12 @@
     for peer in range(1, parts.shape[0]):
         total = total + parts[peer]
     lane = lane_index(total.shape[0])
-    wides = []
-    for method in (core, 1 - core):
+    for place, method in enumerate((core, 1 - core)):
         predicted = jnp.sum(jnp.where(lane == method, total, 0.0), axis=1, keepdims=True) / root_cells
-        wides.append(residual_weights(predicted, stations[method * cell_blocks])[1])
-
-    def body(owner, carry):
+        _, wide[place] = residual_weights(predicted, stations[method * cell_blocks])
+
+    def owner_rows(owner):
+        gradients = []
         for row in range(share):
             sources = (
                 (sens, lanes_of(owner * rows + core * share + row)),
@@ -248,12 +266,12 @@
             for method, (source, lanes) in enumerate(sources):
                 for half in range(halves):
                     at = slice(half * SUB, (half + 1) * SUB)
-                    g = source[at, lanes] * wides[method][at]
+                    g = source[at, lanes] * wide[method, at, :]
                     gradient = g if gradient is None else gradient + g
-            store_row(out, owner * share + row, gradient)
-        return carry
-
-    lax.fori_loop(0, owners, body, 0, unroll=4)
+            gradients.append(gradient)
+        return gradients
+
+    store_tiles(owners, share, owner_rows, out)
 
 
 def second_step_kernel(owners, root_stations, received, own, out):
@@ -313,7 +331,7 @@
         return lax.all_to_all(array, axes, 0, 0, tiled=True)
 
     def swap_rows(array):
-        return swap(array.reshape(owners, 1, -1), "sta").reshape(array.shape)
+        return swap(array.reshape(owners, 1, -1), "sta").reshape(-1, LANES)
 
     parts_shape = (peers, stations, LANES)
     first, sens, send = kernel_call(
@@ -334,8 +352,9 @@
     (terms,) = kernel_call(
         functools.partial(first_terms_kernel, rows, owners, cell_blocks, root_cells),
         "first_terms",
-        [(owners * 3 * share, LANES)],
+        [(owners * 3 * share // SUB, SUB, LANES)],
         [first, sens, got],
+        scratch=[pltpu.VMEM((4, stations, LANES), jnp.float32)],
     )
     own, maxima = kernel_call(
         functools.partial(owner_sum_kernel, rows, owners),
@@ -359,8 +378,9 @@
     (terms,) = kernel_call(
         functools.partial(second_terms_kernel, rows, owners, cell_blocks, root_cells),
         "second_terms",
-        [(owners * share, LANES)],
+        [(owners * share // SUB, SUB, LANES)],
         [swap(second, ("phys", "cell")), first, sens, got],
+        scratch=[pltpu.VMEM((2, stations, LANES), jnp.float32)],
     )
     (halves,) = kernel_call(
         functools.partial(second_step_kernel, owners, root_stations),

time: 103 us -> 101 us (0.981)
  Pallas kernels: 6.72 us -> 4.4 us
    pallas_call x8, Pallas kernels: 6.72 us -> 4.4 us  [kernel_call(): pl.pallas_call(kernel, name=name, out_shape=[make(shape, jnp.float32) for...]
where the time goes in v5:
time: 101 us; the launch traced here: 100 us
  blocking collectives  85.8 us (85%)
  starting transfers between devices  8.79 us (9%)
  Pallas kernels  4.4 us (4%)
  between operations  1.32 us (1%)
    all_to_all x6, blocking collectives, swap(): return lax.all_to_all(array, axes, 0, 0, tiled=True)  82.8 us
    ppermute x1, starting transfers between devices, per_device(): got = lax.ppermute(send, 'phys', [(0, 1), (1, 0)])  8.79 us
    pallas_call x8, Pallas kernels, kernel_call(): pl.pallas_call(kernel, name=name, out_shape=[make(shape, jnp.float32) for...  4.4 us
    all_gather x1, blocking collectives, per_device(): lax.all_gather(halves, 'phys')  3.03 us
  transfers between devices with their start and end apart: 1, of which 0 were waited for; matrix products, arithmetic and copies ran while one was open for 0% of the time, Pallas kernels for 0%

profile of v5, /device:TPU:1, one launch (start us, length us, event | category | flops | bytes accessed | tf_op | source)
XLA Modules:
  0.0 100.4 jit_solution(2276823729262591851)
XLA Ops:
  1.3 1.9 %predict.1 = (f32[8,16,128]{2,1,0:T(8,128)S(1)}, f32[16,32768]{1,0:T(8,128)S(1)}, f32[16,16384]{1,0:T(8,128)S(1)}) custom-call(f32[16,32768]{1,0:T(8,128)} %bitcast.18, f32[256,128]{1,0:T(8,128)} %bitcast.13, f32[1,16]{1,0:T(1,128)} %observed_hbm.1, f32[1,16]{1,0:T(1,128)} %weight_hbm.1, f32[1]{0:T(128)S(6)} %copy.11.scale), custom_call_target="tpu_custom_call" | custom-call | tf_op jit(solution)/shard_map/predict/pallas_call | solution.py:304
  3.1 8.8 %collective-permute-start = (f32[16,16384]{1,0:T(8,128)S(1)}, f32[16,16384]{1,0:T(8,128)S(1)}, u32[]{:S(2)}, u32[]{:S(2)}) collective-permute-start(f32[16,16384]{1,0:T(8,128)S(1)} %get-tuple-element.12), channel_id=1, source_target_pairs={{0,256},{256,0},{1,257},{257,1},{2,258},{258,2},{3,259},{259,3},{4... | collective-permute-start | bytes 3145736 | tf_op jit(solution)/shard_map/ppermute | solution.py:350
  11.9 7.3 %all_to_all.30.parts.stations = f32[8,16,128]{2,1,0:T(8,128)S(1)} all-to-all(f32[8,16,128]{2,1,0:T(8,128)S(1)} %get-tuple-element.10), channel_id=1, replica_groups=mesh['phys'=2,'sta'=64,'cell'=4] {'phys','cell'}, dimensions={0} | all-to-all | bytes 131072 | tf_op jit(solution)/shard_map/all_to_all | solution.py:331
  19.3 0.0 collective-permute-done.got
  19.3 0.0 copy-start
  19.3 0.8 first_terms.1
  20.1 24.7 %all_to_all.31 = f32[64,1,768]{2,1,0:T(1,128)S(1)} all-to-all(f32[64,1,768]{2,1,0:T(1,128)S(1)} %bitcast.12), channel_id=1, replica_groups=mesh['phys'=2,'sta'=64,'cell'=4] {'sta'}, dimensions={0} | all-to-all | bytes 393216 | tf_op jit(solution)/shard_map/all_to_all | solution.py:331
  44.8 0.1 owner_sum.1
  44.9 9.4 %all_to_all.32.maxima = f32[8,1,128]{2,1,0:T(1,128)S(1)} all-to-all(f32[8,1,128]{2,1,0:T(1,128)S(1)} %get-tuple-element.13), channel_id=1, replica_groups=mesh['phys'=2,'sta'=64,'cell'=4] {'phys','cell'}, dimensions={0} | all-to-all | bytes 8192 | tf_op jit(solution)/shard_map/all_to_all | solution.py:331
  54.4 16.4 %all_to_all.33 = f32[64,1,896]{2,1,0:T(1,128)S(1)} all-to-all(f32[64,1,896]{2,1,0:T(1,128)S(1)} %bitcast.9), channel_id=1, replica_groups=mesh['phys'=2,'sta'=64,'cell'=4] {'sta'}, dimensions={0} | all-to-all | bytes 458752 | tf_op jit(solution)/shard_map/all_to_all | solution.py:331
  70.7 0.0 copy-done
  70.8 0.5 model.1
  71.3 10.1 %all_to_all.34.parts = f32[8,16,128]{2,1,0:T(8,128)S(1)} all-to-all(f32[8,16,128]{2,1,0:T(8,128)S(1)} %get-tuple-element.15), channel_id=1, replica_groups=mesh['phys'=2,'sta'=64,'cell'=4] {'phys','cell'}, dimensions={0} | all-to-all | bytes 131072 | tf_op jit(solution)/shard_map/all_to_all | solution.py:331
  81.3 0.5 second_terms.1
  81.8 14.9 %all_to_all.35 = f32[64,1,256]{2,1,0:T(1,128)S(1)} all-to-all(f32[64,1,256]{2,1,0:T(1,128)S(1)} %bitcast.15), channel_id=1, replica_groups=mesh['phys'=2,'sta'=64,'cell'=4] {'sta'}, dimensions={0} | all-to-all | bytes 131072 | tf_op jit(solution)/shard_map/all_to_all | solution.py:331
  96.7 3.0 %all-gather.1.both = f32[2,6,128]{2,1,0:T(8,128)S(1)} all-gather(f32[1,6,128]{2,1,0:T(8,128)S(1)} %bitcast.17), channel_id=2, replica_groups=mesh['phys'=2,'sta'=64,'cell'=4] {'phys'}, dimensions={0}, use_global_device_ids=true | all-gather | bytes 9216 | tf_op jit(solution)/shard_map/all_gather | solution.py:392
  99.8 0.6 layout.1
  (2 shorter events, 0.0 us)
Async XLA Ops:
  3.1 16.1 %collective-permute-start = (f32[16,16384]{1,0:T(8,128)S(1)}, f32[16,16384]{1,0:T(8,128)S(1)}, u32[]{:S(2)}, u32[]{:S(2)}) collective-permute-start(f32[16,16384]{1,0:T(8,128)S(1)} %get-tuple-element.12), channel_id=1, source_target_pairs={{0,256},{256,0},{1,257},{257,1},{2,258},{258,2},{3,259},{259,3},{4... | collective-permute-start | bytes 3145736 | tf_op jit(solution)/shard_map/ppermute | solution.py:350
  19.3 51.5 %copy-start = (f32[32768]{0:T(1024)S(1)}, f32[32768]{0:T(1024)}, u32[]{:S(2)}) copy-start(f32[32768]{0:T(1024)} %param.9) | copy-start | bytes 393220

commit v6 on v5

--- a/solution.py
+++ b/solution.py
@@ -64,12 +64,10 @@
 
 
 def predict_kernel(
-    rows, sens_hbm, model_hbm, observed_hbm, weight_hbm, scale, out, sens, send, model, observed, weight, sems
+    rows, sens_hbm, model_hbm, observed_hbm, weight_hbm, scale, out, sens, model, observed, weight, sems
 ):
     halves, pieces = sens.shape[0] // SUB, sems.shape[0] - 3
     size = sens.shape[1] // pieces
-    share = rows // 2
-    core = lax.axis_index("phys")
     small = [
         pltpu.make_async_copy(source, target, sems.at[pieces + at])
         for at, (source, target) in enumerate(
@@ -96,9 +94,6 @@
             for half in range(halves):
                 slot = (row % 4) * halves + half
                 acc[slot] = acc[slot] + sens[half * SUB : (half + 1) * SUB, lanes_of(at)] * value
-        for row in range(share):
-            source = lanes_of(owner * rows + (1 - core) * share + row)
-            send[:, lanes_of(owner * share + row)] = sens[:, source]
         return tuple(acc)
 
     acc = (jnp.zeros((SUB, LANES), jnp.float32),) * (4 * halves)
@@ -139,12 +134,9 @@
     def owner_rows(owner):
         columns, gradients = ([], []), []
         for row in range(share):
-            sources = (
-                (sens, lanes_of(owner * rows + core * share + row)),
-                (got, lanes_of(owner * share + row)),
-            )
+            lanes = lanes_of(owner * rows + core * share + row)
             gradient = None
-            for method, (source, lanes) in enumerate(sources):
+            for method, source in enumerate((sens, got)):
                 column = None
                 for half in range(halves):
                     at = slice(half * SUB, (half + 1) * SUB)
@@ -160,34 +152,39 @@
     store_tiles(owners, 3 * share, owner_rows, out)
 
 
-def owner_sum_kernel(rows, owners, received, own, out):
+def owner_sum_kernel(rows, owners, received, out):
     share = rows // 2
     core = lax.axis_index("phys")
     size = 3 * share
-    for row in range(size):
-        own[row : row + 1, :] = jnp.sum(received[pl.ds(row, owners, stride=size), :], axis=0, keepdims=True)
+    sums = [jnp.sum(received[pl.ds(row, owners, stride=size), :], axis=0, keepdims=True) for row in range(size)]
+    mine, other, gradient = sums[:share], sums[share : 2 * share], sums[2 * share :]
+    columns = [jnp.where(core == 0, a, b) for a, b in zip(mine + other, other + mine)]
     largest = []
     for method in range(2):
-        most = jnp.max(own[method * share : (method + 1) * share, :], axis=0, keepdims=True)
+        most = functools.reduce(jnp.maximum, columns[method * share : (method + 1) * share])
         largest.append(jnp.max(most, axis=1, keepdims=True))
-    first = jnp.where(core == 0, largest[0], largest[1])
-    second = jnp.where(core == 0, largest[1], largest[0])
-    tile = jnp.where(lane_index(1) < LANES // 2, first, second)
+    most = jnp.where(lane_index(1) < LANES // 2, largest[0], largest[1])
+    fill = [jnp.zeros((out.shape[1] - size - 1, LANES), jnp.float32)] if out.shape[1] > size + 1 else []
+    tile = jnp.concatenate(columns + gradient + [most] + fill, axis=0)
     for peer in range(out.shape[0]):
         out[peer] = tile
 
 
-def message_kernel(owners, maxima, own, out):
-    size = own.shape[0] + 1
-    most = maxima[0]
-    for peer in range(1, maxima.shape[0]):
-        most = jnp.maximum(most, maxima[peer])
+def message_kernel(rows, owners, cell_blocks, slices, out):
+    size = 3 * (rows // 2) + 1
+    core = lax.axis_index("phys")
+    own = slices[core * cell_blocks + lax.axis_index("cell")]
+    most = slices[0, size - 1 : size, :]
+    for peer in range(1, slices.shape[0]):
+        most = jnp.maximum(most, slices[peer, size - 1 : size, :])
     for row in range(size):
-        value = own[row : row + 1, :] if row < size - 1 else most
+        value = own[row : row + 1] if row < size - 1 else most
         out[pl.ds(row, owners, stride=size), :] = jnp.broadcast_to(value, (owners, LANES))
 
 
-def model_kernel(rows, owners, physics, root_stations, message, start, sens, got, out, own, model, weights):
+def model_kernel(
+    rows, owners, cell_blocks, physics, root_stations, message, slices, start, sens, got, out, own, model
+):
     halves = sens.shape[0] // SUB
     share = rows // 2
     core = lax.axis_index("phys")
@@ -196,32 +193,39 @@
     most = jnp.max(message[pl.ds(size - 1, owners, stride=size), :], axis=0, keepdims=True)
     first_lanes = lane_index(1) < LANES // 2
     scales = []
-    for method in (core, 1 - core):
-        inside = first_lanes == (method == 0)
+    for inside in (first_lanes, ~first_lanes):
         largest = jnp.max(jnp.where(inside, most, 0.0), axis=1, keepdims=True)
         scales.append(1.0 / (largest + epsilon))
-    for row in range(share):
+
+    def step(before, columns, summed):
         relative = None
-        for method in range(2):
-            column = message[pl.ds(method * share + row, owners, stride=size), :]
-            r = jnp.sqrt(column * scales[method])
+        for column, scale in zip(columns, scales):
+            r = jnp.sqrt(column * scale)
             relative = r if relative is None else relative + r
         weight = weight_floor + relative / physics
+        return weight, before - step_size * (summed / (root_stations * weight))
+
+    for row in range(share):
+        columns = [message[pl.ds(method * share + row, owners, stride=size), :] for method in range(2)]
         summed = message[pl.ds(2 * share + row, owners, stride=size), :]
         before = [start[pl.ds(at * share + row, owners, stride=rows), :] for at in range(2)]
-        at = pl.ds(row, owners, stride=share)
-        model[at, :] = jnp.where(core == 0, before[0], before[1]) - step_size * (summed / (root_stations * weight))
-        weights[at, :] = weight
+        before = jnp.where(core == 0, before[0], before[1])
+        model[pl.ds(row, owners, stride=share), :] = step(before, columns, summed)[1]
+
+    before = start[pl.ds(position * rows, rows), :]
+    for half in range(2):
+        place = half * cell_blocks + lax.axis_index("cell")
+        columns = [slices[place, method * share : (method + 1) * share, :] for method in range(2)]
+        summed = slices[place, 2 * share : 3 * share, :]
+        at = slice(half * share, (half + 1) * share)
+        own[0, at, :], own[1, at, :] = step(before[at], columns, summed)
 
     def body(owner, acc):
         acc = list(acc)
         for row in range(share):
             value = model[pl.ds(owner * share + row, 1), :]
-            sources = (
-                (sens, lanes_of(owner * rows + core * share + row)),
-                (got, lanes_of(owner * share + row)),
-            )
-            for method, (source, lanes) in enumerate(sources):
+            lanes = lanes_of(owner * rows + core * share + row)
+            for method, source in enumerate((sens, got)):
                 for half in range(halves):
                     slot = ((row % 2) * 2 + method) * halves + half
                     acc[slot] = acc[slot] + source[half * SUB : (half + 1) * SUB, lanes] * value
@@ -238,14 +242,10 @@
     tile = jnp.where(lane == core, columns[0], jnp.where(lane == 1 - core, columns[1], 0.0))
     for peer in range(out.shape[0]):
         out[peer] = tile
-    own_rows = pl.ds(position * share, share)
-    own[0] = weights[own_rows, :]
-    own[1] = model[own_rows, :]
 
 
 def second_terms_kernel(rows, owners, cell_blocks, root_cells, parts, stations, sens, got, out, wide):
     halves = sens.shape[0] // SUB
-    share = rows // 2
     core = lax.axis_index("phys")
     total = parts[0]
     for peer in range(1, parts.shape[0]):
@@ -257,13 +257,10 @@
 
     def owner_rows(owner):
         gradients = []
-        for row in range(share):
-            sources = (
-                (sens, lanes_of(owner * rows + core * share + row)),
-                (got, lanes_of(owner * share + row)),
-            )
+        for row in range(rows):
+            lanes = lanes_of(owner * rows + row)
             gradient = None
-            for method, (source, lanes) in enumerate(sources):
+            for method, source in enumerate((sens, got)):
                 for half in range(halves):
                     at = slice(half * SUB, (half + 1) * SUB)
                     g = source[at, lanes] * wide[method, at, :]
@@ -271,28 +268,19 @@
             gradients.append(gradient)
         return gradients
 
-    store_tiles(owners, share, owner_rows, out)
-
-
-def second_step_kernel(owners, root_stations, received, own, out):
-    share = own.shape[1]
-    for row in range(share):
-        total = jnp.sum(received[pl.ds(row, owners, stride=share), :], axis=0, keepdims=True)
+    store_tiles(owners, rows, owner_rows, out)
+
+
+def second_step_kernel(owners, root_stations, received, own, weight_out, gradient_out, model_out):
+    rows = own.shape[1]
+    for row in range(rows):
+        total = jnp.sum(received[pl.ds(row, owners, stride=rows), :], axis=0, keepdims=True)
         weight = own[0, row : row + 1, :]
         gradient = total / (root_stations * weight)
-        out[row : row + 1, :] = weight
-        out[share + row : share + row + 1, :] = gradient
-        out[2 * share + row : 2 * share + row + 1, :] = own[1, row : row + 1, :] - step_size * gradient
-
-
-def layout_kernel(both, *outs):
-    share = both.shape[1] // len(outs)
-    for at, out in enumerate(outs):
-        for core in range(both.shape[0]):
-            for row in range(share):
-                to = (core * share + row) * LANES
-                source = at * share + row
-                out[:, to : to + LANES] = both[core, source : source + 1, :]
+        lanes = slice(row * LANES, (row + 1) * LANES)
+        weight_out[:, lanes] = weight
+        gradient_out[:, lanes] = gradient
+        model_out[:, lanes] = own[1, row : row + 1, :] - step_size * gradient
 
 
 def kernel_call(kernel, name, outs, operands, scratch=(), spaces=None, kept=True):
@@ -334,10 +322,10 @@
         return swap(array.reshape(owners, 1, -1), "sta").reshape(-1, LANES)
 
     parts_shape = (peers, stations, LANES)
-    first, sens, send = kernel_call(
+    first, sens = kernel_call(
         functools.partial(predict_kernel, rows),
         "predict",
-        [parts_shape, (stations, cell_count), (stations, cell_count // 2)],
+        [parts_shape, (stations, cell_count)],
         [sens, start, observed, data_weight, phys_weight],
         scratch=[
             pltpu.VMEM((chunks, LANES), jnp.float32),
@@ -347,7 +335,7 @@
         ],
         spaces=[pltpu.HBM] * 4 + [pltpu.SMEM],
     )
-    got = lax.ppermute(send, "phys", [(0, 1), (1, 0)])
+    got = lax.ppermute(sens, "phys", [(0, 1), (1, 0)])
     first = swap(first, ("phys", "cell"))
     (terms,) = kernel_call(
         functools.partial(first_terms_kernel, rows, owners, cell_blocks, root_cells),
@@ -356,40 +344,42 @@
         [first, sens, got],
         scratch=[pltpu.VMEM((4, stations, LANES), jnp.float32)],
     )
-    own, maxima = kernel_call(
+    size = 3 * share + 1
+    (slices,) = kernel_call(
         functools.partial(owner_sum_kernel, rows, owners),
         "owner_sum",
-        [(3 * share, LANES), (peers, 1, LANES)],
+        [(peers, -(-size // SUB) * SUB, LANES)],
         [swap_rows(terms)],
     )
+    slices = swap(slices, ("phys", "cell"))
     (message,) = kernel_call(
-        functools.partial(message_kernel, owners),
+        functools.partial(message_kernel, rows, owners, cell_blocks),
         "message",
-        [(owners * (3 * share + 1), LANES)],
-        [swap(maxima, ("phys", "cell")), own],
+        [(owners * size, LANES)],
+        [slices],
     )
     second, own = kernel_call(
-        functools.partial(model_kernel, rows, owners, physics, root_stations),
+        functools.partial(model_kernel, rows, owners, cell_blocks, physics, root_stations),
         "model",
-        [parts_shape, (2, share, LANES)],
-        [swap_rows(message), start, sens, got],
-        scratch=[pltpu.VMEM((chunks // 2, LANES), jnp.float32)] * 2,
+        [parts_shape, (2, rows, LANES)],
+        [swap_rows(message), slices, start, sens, got],
+        scratch=[pltpu.VMEM((chunks // 2, LANES), jnp.float32)],
     )
     (terms,) = kernel_call(
         functools.partial(second_terms_kernel, rows, owners, cell_blocks, root_cells),
         "second_terms",
-        [(owners * share // SUB, SUB, LANES)],
+        [(chunks // SUB, SUB, LANES)],
         [swap(second, ("phys", "cell")), first, sens, got],
         scratch=[pltpu.VMEM((2, stations, LANES), jnp.float32)],
     )
-    (halves,) = kernel_call(
-        functools.partial(second_step_kernel, owners, root_stations),
-        "second_step",
-        [(3 * share, LANES)],
-        [swap_rows(terms), own],
-    )
     return tuple(
-        kernel_call(layout_kernel, "layout", [(1, rows * LANES)] * 3, [lax.all_gather(halves, "phys")], kept=False)
+        kernel_call(
+            functools.partial(second_step_kernel, owners, root_stations),
+            "second_step",
+            [(1, rows * LANES)] * 3,
+            [swap_rows(terms), own],
+            kept=False,
+        )
     )
 
 

time: 101 us -> 98.9 us (0.979)
  blocking collectives: 85.8 us -> 83.7 us
    all_gather x1 -> x0, blocking collectives: 3.03 us -> none  [per_device(): lax.all_gather(halves, 'phys')]
    pallas_call x8 -> x7, Pallas kernels: 4.4 us -> 4.66 us  [kernel_call(): pl.pallas_call(kernel, name=name, out_shape=[make(shape, jnp.float32) for...]
where the time goes in v6:
time: 98.9 us; the launch traced here: 98.5 us
  blocking collectives  83.7 us (85%)
  starting transfers between devices  8.79 us (9%)
  Pallas kernels  4.66 us (5%)
  between operations  1.32 us (1%)
    all_to_all x6, blocking collectives, swap(): return lax.all_to_all(array, axes, 0, 0, tiled=True)  83.7 us
    ppermute x1, starting transfers between devices, per_device(): got = lax.ppermute(sens, 'phys', [(0, 1), (1, 0)])  8.79 us
    pallas_call x7, Pallas kernels, kernel_call(): pl.pallas_call(kernel, name=name, out_shape=[make(shape, jnp.float32) for...  4.66 us
  transfers between devices with their start and end apart: 1, of which 0 were waited for; matrix products, arithmetic and copies ran while one was open for 0% of the time, Pallas kernels for 0%

profile of v6, /device:TPU:1, one launch (start us, length us, event | category | flops | bytes accessed | tf_op | source)
XLA Modules:
  0.0 98.5 jit_solution(14765993380710277035)
XLA Ops:
  1.3 1.9 %predict.1 = (f32[8,16,128]{2,1,0:T(8,128)S(1)}, f32[16,32768]{1,0:T(8,128)S(1)}) custom-call(f32[16,32768]{1,0:T(8,128)} %bitcast.16, f32[256,128]{1,0:T(8,128)} %bitcast.12, f32[1,16]{1,0:T(1,128)} %observed_hbm.1, f32[1,16]{1,0:T(1,128)} %weight_hbm.1, f32[1]{0:T(128)S(6)} %copy.11.scale), custom_call_target="tpu_custom_call" | custom-call | tf_op jit(solution)/shard_map/predict/pallas_call | solution.py:292
  3.1 8.8 %collective-permute-start = (f32[16,32768]{1,0:T(8,128)S(1)}, f32[16,32768]{1,0:T(8,128)S(1)}, u32[]{:S(2)}, u32[]{:S(2)}) collective-permute-start(f32[16,32768]{1,0:T(8,128)S(1)} %get-tuple-element.8.sens), channel_id=1, source_target_pairs={{0,256},{256,0},{1,257},{257,1},{2,258},{258,2},{3,259},{259,3},{4... | collective-permute-start | bytes 6291464 | tf_op jit(solution)/shard_map/ppermute | solution.py:338
  11.9 7.3 %all_to_all.30.parts.stations = f32[8,16,128]{2,1,0:T(8,128)S(1)} all-to-all(f32[8,16,128]{2,1,0:T(8,128)S(1)} %get-tuple-element.7), channel_id=1, replica_groups=mesh['phys'=2,'sta'=64,'cell'=4] {'phys','cell'}, dimensions={0} | all-to-all | bytes 131072 | tf_op jit(solution)/shard_map/all_to_all | solution.py:319
  19.3 0.0 copy-start
  19.3 0.0 collective-permute-done.got
  19.3 0.8 first_terms.1
  20.1 24.7 %all_to_all.31 = f32[64,1,768]{2,1,0:T(1,128)S(1)} all-to-all(f32[64,1,768]{2,1,0:T(1,128)S(1)} %bitcast.10), channel_id=1, replica_groups=mesh['phys'=2,'sta'=64,'cell'=4] {'sta'}, dimensions={0} | all-to-all | bytes 393216 | tf_op jit(solution)/shard_map/all_to_all | solution.py:319
  44.8 0.1 owner_sum.1
  44.9 9.8 %all_to_all.32.slices = f32[8,8,128]{2,1,0:T(8,128)S(1)} all-to-all(f32[8,8,128]{2,1,0:T(8,128)S(1)} %owner_sum.1), channel_id=1, replica_groups=mesh['phys'=2,'sta'=64,'cell'=4] {'phys','cell'}, dimensions={0} | all-to-all | bytes 65536 | tf_op jit(solution)/shard_map/all_to_all | solution.py:319
  54.7 16.8 %all_to_all.33 = f32[64,1,896]{2,1,0:T(1,128)S(1)} all-to-all(f32[64,1,896]{2,1,0:T(1,128)S(1)} %bitcast.8), channel_id=1, replica_groups=mesh['phys'=2,'sta'=64,'cell'=4] {'sta'}, dimensions={0} | all-to-all | bytes 458752 | tf_op jit(solution)/shard_map/all_to_all | solution.py:319
  71.5 0.0 copy-done
  71.5 0.6 model.1
  72.1 9.7 %all_to_all.34.parts = f32[8,16,128]{2,1,0:T(8,128)S(1)} all-to-all(f32[8,16,128]{2,1,0:T(8,128)S(1)} %get-tuple-element.9), channel_id=1, replica_groups=mesh['phys'=2,'sta'=64,'cell'=4] {'phys','cell'}, dimensions={0} | all-to-all | bytes 131072 | tf_op jit(solution)/shard_map/all_to_all | solution.py:319
  81.8 0.7 second_terms.1
  82.5 15.4 %all_to_all.35 = f32[64,1,512]{2,1,0:T(1,128)S(1)} all-to-all(f32[64,1,512]{2,1,0:T(1,128)S(1)} %bitcast.14), channel_id=1, replica_groups=mesh['phys'=2,'sta'=64,'cell'=4] {'sta'}, dimensions={0} | all-to-all | bytes 262144 | tf_op jit(solution)/shard_map/all_to_all | solution.py:319
  97.9 0.6 second_step.1
  (1 shorter events, 0.0 us)
Async XLA Ops:
  3.1 16.1 %collective-permute-start = (f32[16,32768]{1,0:T(8,128)S(1)}, f32[16,32768]{1,0:T(8,128)S(1)}, u32[]{:S(2)}, u32[]{:S(2)}) collective-permute-start(f32[16,32768]{1,0:T(8,128)S(1)} %get-tuple-element.8.sens), channel_id=1, source_target_pairs={{0,256},{256,0},{1,257},{257,1},{2,258},{258,2},{3,259},{259,3},{4... | collective-permute-start | bytes 6291464 | tf_op jit(solution)/shard_map/ppermute | solution.py:338
  19.3 52.2 %copy-start = (f32[32768]{0:T(1024)S(1)}, f32[32768]{0:T(1024)}, u32[]{:S(2)}) copy-start(f32[32768]{0:T(1024)} %param.9) | copy-start | bytes 393220

commit v7 on v6

--- a/solution.py
+++ b/solution.py
@@ -15,6 +15,30 @@
 step_size = 0.5
 weight_floor = 0.1
 epsilon = 1e-06
+
+RANK_BITS = (0, 2, 3, 5, 4, 1)
+
+
+def bit_names(owners):
+    return tuple(f"sta_{bit}" for bit in range(owners.bit_length() - 1))
+
+
+def rank_bits(owners):
+    bits = range(len(bit_names(owners)))
+    return RANK_BITS if len(RANK_BITS) == len(bits) else tuple(bits)
+
+
+def owner_of_rank(owners):
+    bits = rank_bits(owners)
+    last = len(bits) - 1
+    return [sum((rank >> (last - at) & 1) << (last - bit) for at, bit in enumerate(bits)) for rank in range(owners)]
+
+
+def sta_index(owners):
+    index = 0
+    for name in bit_names(owners):
+        index = index * 2 + lax.axis_index(name)
+    return index
 
 
 def lane_index(rows):
@@ -52,13 +76,14 @@
 
 
 def store_tiles(owners, size, owner_rows, out):
+    places = owner_of_rank(owners)
     group = SUB // math.gcd(SUB, size)
     tiles = group * size // SUB
 
     for step in range(owners // group):
         values = []
         for member in range(group):
-            values += owner_rows(step * group + member)
+            values += owner_rows(places[step * group + member])
         for tile in range(tiles):
             out[step * tiles + tile] = fold(values[tile * SUB : (tile + 1) * SUB])
 
@@ -188,7 +213,8 @@
     halves = sens.shape[0] // SUB
     share = rows // 2
     core = lax.axis_index("phys")
-    position = lax.axis_index("sta")
+    position = sta_index(owners)
+    places = owner_of_rank(owners)
     size = message.shape[0] // owners
     most = jnp.max(message[pl.ds(size - 1, owners, stride=size), :], axis=0, keepdims=True)
     first_lanes = lane_index(1) < LANES // 2
@@ -205,12 +231,14 @@
         weight = weight_floor + relative / physics
         return weight, before - step_size * (summed / (root_stations * weight))
 
+    for rank, owner in enumerate(places):
+        before = [start[owner * rows + half * share : owner * rows + (half + 1) * share, :] for half in range(2)]
+        model[rank * share : (rank + 1) * share, :] = jnp.where(core == 0, before[0], before[1])
     for row in range(share):
         columns = [message[pl.ds(method * share + row, owners, stride=size), :] for method in range(2)]
         summed = message[pl.ds(2 * share + row, owners, stride=size), :]
-        before = [start[pl.ds(at * share + row, owners, stride=rows), :] for at in range(2)]
-        before = jnp.where(core == 0, before[0], before[1])
-        model[pl.ds(row, owners, stride=share), :] = step(before, columns, summed)[1]
+        at = pl.ds(row, owners, stride=share)
+        model[at, :] = step(model[at, :], columns, summed)[1]
 
     before = start[pl.ds(position * rows, rows), :]
     for half in range(2):
@@ -220,11 +248,11 @@
         at = slice(half * share, (half + 1) * share)
         own[0, at, :], own[1, at, :] = step(before[at], columns, summed)
 
-    def body(owner, acc):
+    def body(rank, acc):
         acc = list(acc)
         for row in range(share):
-            value = model[pl.ds(owner * share + row, 1), :]
-            lanes = lanes_of(owner * rows + core * share + row)
+            value = model[pl.ds(rank * share + row, 1), :]
+            lanes = lanes_of(places[rank] * rows + core * share + row)
             for method, source in enumerate((sens, got)):
                 for half in range(halves):
                     slot = ((row % 2) * 2 + method) * halves + half
@@ -232,8 +260,8 @@
         return tuple(acc)
 
     acc = (jnp.zeros((SUB, LANES), jnp.float32),) * (4 * halves)
-    for owner in range(owners):
-        acc = body(owner, acc)
+    for rank in range(owners):
+        acc = body(rank, acc)
     columns = []
     for method in range(2):
         total = [acc[method * halves + half] + acc[(2 + method) * halves + half] for half in range(halves)]
@@ -300,8 +328,8 @@
     )(*operands)
 
 
-def per_device(sensitivity, observed, data_weight, phys_weight, start_model):
-    owners = lax.axis_size("sta")
+def per_device(sta, sensitivity, observed, data_weight, phys_weight, start_model):
+    owners = math.prod(lax.axis_size(name) for name in sta)
     cell_blocks = lax.axis_size("cell")
     physics = sensitivity.shape[0] * lax.axis_size("phys")
     stations, cell_count = sensitivity.shape[1:]
@@ -319,7 +347,7 @@
         return lax.all_to_all(array, axes, 0, 0, tiled=True)
 
     def swap_rows(array):
-        return swap(array.reshape(owners, 1, -1), "sta").reshape(-1, LANES)
+        return swap(array.reshape(owners, 1, -1), tuple(sta[bit] for bit in rank_bits(owners))).reshape(-1, LANES)
 
     parts_shape = (peers, stations, LANES)
     first, sens = kernel_call(
@@ -384,16 +412,21 @@
 
 
 def solution(mesh):
+    owners = mesh.shape["sta"]
+    sta = bit_names(owners)
+    split = jax.sharding.Mesh(
+        mesh.devices.reshape((mesh.shape["phys"],) + (2,) * len(sta) + (mesh.shape["cell"],)), ("phys",) + sta + ("cell",)
+    )
     return jax.shard_map(
-        per_device,
-        mesh=mesh,
+        functools.partial(per_device, sta),
+        mesh=split,
         in_specs=(
-            P("phys", "sta", "cell"),
-            P("phys", "sta"),
-            P("phys", "sta"),
+            P("phys", sta, "cell"),
+            P("phys", sta),
+            P("phys", sta),
             P("phys"),
             P("cell"),
         ),
-        out_specs=(P("cell", "sta"), P("cell", "sta"), P("cell", "sta")),
+        out_specs=(P("cell", sta),) * 3,
         check_vma=False,
     )

time: 98.9 us -> 97.9 us (0.990)
  blocking collectives: 83.7 us -> 82.7 us
    all_to_all x6, blocking collectives: 83.7 us -> 82.7 us  [swap(): return lax.all_to_all(array, axes, 0, 0, tiled=True)]
where the time goes in v7:
time: 97.9 us; the launch traced here: 97.5 us
  blocking collectives  82.7 us (84%)
  starting transfers between devices  8.79 us (9%)
  Pallas kernels  4.68 us (5%)
  between operations  1.32 us (1%)
    all_to_all x6, blocking collectives, swap(): return lax.all_to_all(array, axes, 0, 0, tiled=True)  82.7 us
    ppermute x1, starting transfers between devices, per_device(): got = lax.ppermute(sens, 'phys', [(0, 1), (1, 0)])  8.79 us
    pallas_call x7, Pallas kernels, kernel_call(): pl.pallas_call(kernel, name=name, out_shape=[make(shape, jnp.float32) for...  4.68 us
  transfers between devices with their start and end apart: 1, of which 0 were waited for; matrix products, arithmetic and copies ran while one was open for 0% of the time, Pallas kernels for 0%

profile of v7, /device:TPU:1, one launch (start us, length us, event | category | flops | bytes accessed | tf_op | source)
XLA Modules:
  0.0 97.5 jit_solution(18093533376012187034)
XLA Ops:
  1.3 1.9 %predict.1 = (f32[8,16,128]{2,1,0:T(8,128)S(1)}, f32[16,32768]{1,0:T(8,128)S(1)}) custom-call(f32[16,32768]{1,0:T(8,128)} %bitcast.16, f32[256,128]{1,0:T(8,128)} %bitcast.12, f32[1,16]{1,0:T(1,128)} %observed_hbm.1, f32[1,16]{1,0:T(1,128)} %weight_hbm.1, f32[1]{0:T(128)S(6)} %copy.11.scale), custom_call_target="tpu_custom_call" | custom-call | tf_op jit(solution)/shard_map/predict/pallas_call | solution.py:320
  3.1 8.8 %collective-permute-start = (f32[16,32768]{1,0:T(8,128)S(1)}, f32[16,32768]{1,0:T(8,128)S(1)}, u32[]{:S(2)}, u32[]{:S(2)}) collective-permute-start(f32[16,32768]{1,0:T(8,128)S(1)} %get-tuple-element.8.sens), channel_id=1, source_target_pairs={{0,256},{256,0},{1,257},{257,1},{2,258},{258,2},{3,259},{259,3},{4... | collective-permute-start | bytes 6291464 | tf_op jit(solution)/shard_map/ppermute | solution.py:366
  11.9 7.3 %all_to_all.30.parts.stations = f32[8,16,128]{2,1,0:T(8,128)S(1)} all-to-all(f32[8,16,128]{2,1,0:T(8,128)S(1)} %get-tuple-element.7), channel_id=1, replica_groups=mesh['phys'=2,'sta_0'=2,'sta_1'=2,'sta_2'=2,'sta_3'=2,'sta_4'=2,'sta_5'=..., dimensions={0} | all-to-all | bytes 131072 | tf_op jit(solution)/shard_map/all_to_all | solution.py:347
  19.3 0.0 copy-start
  19.3 0.0 collective-permute-done.got
  19.3 0.8 first_terms.1
  20.1 24.0 %all_to_all.31 = f32[64,1,768]{2,1,0:T(1,128)S(1)} all-to-all(f32[64,1,768]{2,1,0:T(1,128)S(1)} %bitcast.10), channel_id=1, replica_groups=mesh['phys'=2,'sta_0'=2,'sta_1'=2,'sta_2'=2,'sta_3'=2,'sta_4'=2,'sta_5'=..., dimensions={0} | all-to-all | bytes 393216 | tf_op jit(solution)/shard_map/all_to_all | solution.py:347
  44.0 0.1 owner_sum.1
  44.1 9.8 %all_to_all.32.slices = f32[8,8,128]{2,1,0:T(8,128)S(1)} all-to-all(f32[8,8,128]{2,1,0:T(8,128)S(1)} %owner_sum.1), channel_id=1, replica_groups=mesh['phys'=2,'sta_0'=2,'sta_1'=2,'sta_2'=2,'sta_3'=2,'sta_4'=2,'sta_5'=..., dimensions={0} | all-to-all | bytes 65536 | tf_op jit(solution)/shard_map/all_to_all | solution.py:347
  53.9 15.9 %all_to_all.33 = f32[64,1,896]{2,1,0:T(1,128)S(1)} all-to-all(f32[64,1,896]{2,1,0:T(1,128)S(1)} %bitcast.8), channel_id=1, replica_groups=mesh['phys'=2,'sta_0'=2,'sta_1'=2,'sta_2'=2,'sta_3'=2,'sta_4'=2,'sta_5'=..., dimensions={0} | all-to-all | bytes 458752 | tf_op jit(solution)/shard_map/all_to_all | solution.py:347
  69.8 0.0 copy-done
  69.8 0.6 model.1
  70.5 9.9 %all_to_all.34.parts = f32[8,16,128]{2,1,0:T(8,128)S(1)} all-to-all(f32[8,16,128]{2,1,0:T(8,128)S(1)} %get-tuple-element.9), channel_id=1, replica_groups=mesh['phys'=2,'sta_0'=2,'sta_1'=2,'sta_2'=2,'sta_3'=2,'sta_4'=2,'sta_5'=..., dimensions={0} | all-to-all | bytes 131072 | tf_op jit(solution)/shard_map/all_to_all | solution.py:347
  80.4 0.7 second_terms.1
  81.1 15.8 %all_to_all.35 = f32[64,1,512]{2,1,0:T(1,128)S(1)} all-to-all(f32[64,1,512]{2,1,0:T(1,128)S(1)} %bitcast.14), channel_id=1, replica_groups=mesh['phys'=2,'sta_0'=2,'sta_1'=2,'sta_2'=2,'sta_3'=2,'sta_4'=2,'sta_5'=..., dimensions={0} | all-to-all | bytes 262144 | tf_op jit(solution)/shard_map/all_to_all | solution.py:347
  96.9 0.6 second_step.1
  (1 shorter events, 0.0 us)
Async XLA Ops:
  3.1 16.1 %collective-permute-start = (f32[16,32768]{1,0:T(8,128)S(1)}, f32[16,32768]{1,0:T(8,128)S(1)}, u32[]{:S(2)}, u32[]{:S(2)}) collective-permute-start(f32[16,32768]{1,0:T(8,128)S(1)} %get-tuple-element.8.sens), channel_id=1, source_target_pairs={{0,256},{256,0},{1,257},{257,1},{2,258},{258,2},{3,259},{259,3},{4... | collective-permute-start | bytes 6291464 | tf_op jit(solution)/shard_map/ppermute | solution.py:366
  19.3 50.6 %copy-start = (f32[32768]{0:T(1024)S(1)}, f32[32768]{0:T(1024)}, u32[]{:S(2)}) copy-start(f32[32768]{0:T(1024)} %param.9) | copy-start | bytes 393220

commit v8 on v6

--- a/solution.py
+++ b/solution.py
@@ -15,6 +15,19 @@
 step_size = 0.5
 weight_floor = 0.1
 epsilon = 1e-06
+
+RANK_BITS = (5, 2, 4, 1, 3, 0)
+FIRST = 36
+
+
+def owner_of_rank(owners):
+    count = owners.bit_length() - 1
+    bits = RANK_BITS if len(RANK_BITS) == count else range(count)
+    first = FIRST % owners
+    last = count - 1
+    return [
+        first ^ sum((rank >> (last - at) & 1) << (last - bit) for at, bit in enumerate(bits)) for rank in range(owners)
+    ]
 
 
 def lane_index(rows):
@@ -52,13 +65,14 @@
 
 
 def store_tiles(owners, size, owner_rows, out):
+    places = owner_of_rank(owners)
     group = SUB // math.gcd(SUB, size)
     tiles = group * size // SUB
 
     for step in range(owners // group):
         values = []
         for member in range(group):
-            values += owner_rows(step * group + member)
+            values += owner_rows(places[step * group + member])
         for tile in range(tiles):
             out[step * tiles + tile] = fold(values[tile * SUB : (tile + 1) * SUB])
 
@@ -189,6 +203,7 @@
     share = rows // 2
     core = lax.axis_index("phys")
     position = lax.axis_index("sta")
+    places = owner_of_rank(owners)
     size = message.shape[0] // owners
     most = jnp.max(message[pl.ds(size - 1, owners, stride=size), :], axis=0, keepdims=True)
     first_lanes = lane_index(1) < LANES // 2
@@ -205,12 +220,14 @@
         weight = weight_floor + relative / physics
         return weight, before - step_size * (summed / (root_stations * weight))
 
+    for rank, owner in enumerate(places):
+        before = [start[owner * rows + half * share : owner * rows + (half + 1) * share, :] for half in range(2)]
+        model[rank * share : (rank + 1) * share, :] = jnp.where(core == 0, before[0], before[1])
     for row in range(share):
         columns = [message[pl.ds(method * share + row, owners, stride=size), :] for method in range(2)]
         summed = message[pl.ds(2 * share + row, owners, stride=size), :]
-        before = [start[pl.ds(at * share + row, owners, stride=rows), :] for at in range(2)]
-        before = jnp.where(core == 0, before[0], before[1])
-        model[pl.ds(row, owners, stride=share), :] = step(before, columns, summed)[1]
+        at = pl.ds(row, owners, stride=share)
+        model[at, :] = step(model[at, :], columns, summed)[1]
 
     before = start[pl.ds(position * rows, rows), :]
     for half in range(2):
@@ -220,11 +237,11 @@
         at = slice(half * share, (half + 1) * share)
         own[0, at, :], own[1, at, :] = step(before[at], columns, summed)
 
-    def body(owner, acc):
+    def body(rank, acc):
         acc = list(acc)
         for row in range(share):
-            value = model[pl.ds(owner * share + row, 1), :]
-            lanes = lanes_of(owner * rows + core * share + row)
+            value = model[pl.ds(rank * share + row, 1), :]
+            lanes = lanes_of(places[rank] * rows + core * share + row)
             for method, source in enumerate((sens, got)):
                 for half in range(halves):
                     slot = ((row % 2) * 2 + method) * halves + half
@@ -232,8 +249,8 @@
         return tuple(acc)
 
     acc = (jnp.zeros((SUB, LANES), jnp.float32),) * (4 * halves)
-    for owner in range(owners):
-        acc = body(owner, acc)
+    for rank in range(owners):
+        acc = body(rank, acc)
     columns = []
     for method in range(2):
         total = [acc[method * halves + half] + acc[(2 + method) * halves + half] for half in range(halves)]
@@ -315,11 +332,11 @@
     peers = physics * cell_blocks
     pieces = min(8, owners)
 
-    def swap(array, axes):
-        return lax.all_to_all(array, axes, 0, 0, tiled=True)
+    def swap(array, axes, groups=None):
+        return lax.all_to_all(array, axes, 0, 0, axis_index_groups=groups, tiled=True)
 
     def swap_rows(array):
-        return swap(array.reshape(owners, 1, -1), "sta").reshape(-1, LANES)
+        return swap(array.reshape(owners, 1, -1), "sta", [owner_of_rank(owners)]).reshape(-1, LANES)
 
     parts_shape = (peers, stations, LANES)
     first, sens = kernel_call(
@@ -394,6 +411,6 @@
             P("phys"),
             P("cell"),
         ),
-        out_specs=(P("cell", "sta"), P("cell", "sta"), P("cell", "sta")),
+        out_specs=(P("cell", "sta"),) * 3,
         check_vma=False,
     )

time: 98.9 us -> 92.8 us (0.938)
  blocking collectives: 83.7 us -> 77.7 us
    all_to_all x6, blocking collectives: 83.7 us -> 77.7 us  [swap(): lax.all_to_all(array, axes, 0, 0, axis_index_groups=groups, tiled=True)]
where the time goes in v8:
time: 92.8 us; the launch traced here: 92.4 us
  blocking collectives  77.7 us (84%)
  starting transfers between devices  8.79 us (9%)
  Pallas kernels  4.67 us (5%)
  between operations  1.32 us (1%)
    all_to_all x6, blocking collectives, swap(): lax.all_to_all(array, axes, 0, 0, axis_index_groups=groups, tiled=True)  77.7 us
    ppermute x1, starting transfers between devices, per_device(): got = lax.ppermute(sens, 'phys', [(0, 1), (1, 0)])  8.79 us
    pallas_call x7, Pallas kernels, kernel_call(): pl.pallas_call(kernel, name=name, out_shape=[make(shape, jnp.float32) for...  4.67 us
  transfers between devices with their start and end apart: 1, of which 0 were waited for; matrix products, arithmetic and copies ran while one was open for 0% of the time, Pallas kernels for 0%

profile of v8, /device:TPU:1, one launch (start us, length us, event | category | flops | bytes accessed | tf_op | source)
XLA Modules:
  0.0 92.4 jit_solution(16078743735643402228)
XLA Ops:
  1.3 1.9 %predict.1 = (f32[8,16,128]{2,1,0:T(8,128)S(1)}, f32[16,32768]{1,0:T(8,128)S(1)}) custom-call(f32[16,32768]{1,0:T(8,128)} %bitcast.16, f32[256,128]{1,0:T(8,128)} %bitcast.12, f32[1,16]{1,0:T(1,128)} %observed_hbm.1, f32[1,16]{1,0:T(1,128)} %weight_hbm.1, f32[1]{0:T(128)S(6)} %copy.11.scale), custom_call_target="tpu_custom_call" | custom-call | tf_op jit(solution)/shard_map/predict/pallas_call | solution.py:309
  3.1 8.8 %collective-permute-start = (f32[16,32768]{1,0:T(8,128)S(1)}, f32[16,32768]{1,0:T(8,128)S(1)}, u32[]{:S(2)}, u32[]{:S(2)}) collective-permute-start(f32[16,32768]{1,0:T(8,128)S(1)} %get-tuple-element.8.sens), channel_id=1, source_target_pairs={{0,256},{256,0},{1,257},{257,1},{2,258},{258,2},{3,259},{259,3},{4... | collective-permute-start | bytes 6291464 | tf_op jit(solution)/shard_map/ppermute | solution.py:355
  11.9 7.3 %all_to_all.30.parts.stations = f32[8,16,128]{2,1,0:T(8,128)S(1)} all-to-all(f32[8,16,128]{2,1,0:T(8,128)S(1)} %get-tuple-element.7), channel_id=1, replica_groups=mesh['phys'=2,'sta'=64,'cell'=4] {'phys','cell'}, dimensions={0} | all-to-all | bytes 131072 | tf_op jit(solution)/shard_map/all_to_all | solution.py:336
  19.3 0.0 copy-start
  19.3 0.0 collective-permute-done.got
  19.3 0.8 first_terms.1
  20.1 20.3 %all_to_all.31 = f32[64,1,768]{2,1,0:T(1,128)S(1)} all-to-all(f32[64,1,768]{2,1,0:T(1,128)S(1)} %bitcast.10), channel_id=1, replica_groups={{144,16,128,0,208,80,192,64,152,24,136,8,216,88,200,72,176,48,160,32,24..., dimensions={0} | all-to-all | bytes 393216 | tf_op jit(solution)/shard_map/all_to_all | solution.py:336
  40.4 0.1 owner_sum.1
  40.5 8.5 %all_to_all.32.slices = f32[8,8,128]{2,1,0:T(8,128)S(1)} all-to-all(f32[8,8,128]{2,1,0:T(8,128)S(1)} %owner_sum.1), channel_id=1, replica_groups=mesh['phys'=2,'sta'=64,'cell'=4] {'phys','cell'}, dimensions={0} | all-to-all | bytes 65536 | tf_op jit(solution)/shard_map/all_to_all | solution.py:336
  49.1 17.4 %all_to_all.33 = f32[64,1,896]{2,1,0:T(1,128)S(1)} all-to-all(f32[64,1,896]{2,1,0:T(1,128)S(1)} %bitcast.8), channel_id=1, replica_groups={{144,16,128,0,208,80,192,64,152,24,136,8,216,88,200,72,176,48,160,32,24..., dimensions={0} | all-to-all | bytes 458752 | tf_op jit(solution)/shard_map/all_to_all | solution.py:336
  66.5 0.0 copy-done
  66.5 0.6 model.1
  67.1 8.7 %all_to_all.34.parts = f32[8,16,128]{2,1,0:T(8,128)S(1)} all-to-all(f32[8,16,128]{2,1,0:T(8,128)S(1)} %get-tuple-element.9), channel_id=1, replica_groups=mesh['phys'=2,'sta'=64,'cell'=4] {'phys','cell'}, dimensions={0} | all-to-all | bytes 131072 | tf_op jit(solution)/shard_map/all_to_all | solution.py:336
  75.8 0.7 second_terms.1
  76.5 15.3 %all_to_all.35 = f32[64,1,512]{2,1,0:T(1,128)S(1)} all-to-all(f32[64,1,512]{2,1,0:T(1,128)S(1)} %bitcast.14), channel_id=1, replica_groups={{144,16,128,0,208,80,192,64,152,24,136,8,216,88,200,72,176,48,160,32,24..., dimensions={0} | all-to-all | bytes 262144 | tf_op jit(solution)/shard_map/all_to_all | solution.py:336
  91.8 0.6 second_step.1
  (1 shorter events, 0.0 us)
Async XLA Ops:
  3.1 16.1 %collective-permute-start = (f32[16,32768]{1,0:T(8,128)S(1)}, f32[16,32768]{1,0:T(8,128)S(1)}, u32[]{:S(2)}, u32[]{:S(2)}) collective-permute-start(f32[16,32768]{1,0:T(8,128)S(1)} %get-tuple-element.8.sens), channel_id=1, source_target_pairs={{0,256},{256,0},{1,257},{257,1},{2,258},{258,2},{3,259},{259,3},{4... | collective-permute-start | bytes 6291464 | tf_op jit(solution)/shard_map/ppermute | solution.py:355
  19.3 47.2 %copy-start = (f32[32768]{0:T(1024)S(1)}, f32[32768]{0:T(1024)}, u32[]{:S(2)}) copy-start(f32[32768]{0:T(1024)} %param.9) | copy-start | bytes 393220

commit v9 on v8

--- a/solution.py
+++ b/solution.py
@@ -16,8 +16,8 @@
 weight_floor = 0.1
 epsilon = 1e-06
 
-RANK_BITS = (5, 2, 4, 1, 3, 0)
-FIRST = 36
+RANK_BITS = (5, 2, 4, 1, 0, 3)
+FIRST = 52
 
 
 def owner_of_rank(owners):

time: 92.8 us -> 92.1 us (level)
  no operation moved by 1% of the time
where the time goes in v9:
time: 92.1 us; the launch traced here: 91.6 us
  blocking collectives  76.8 us (83%)
  starting transfers between devices  8.79 us (10%)
  Pallas kernels  4.67 us (5%)
  between operations  1.32 us (1%)
    all_to_all x6, blocking collectives, swap(): lax.all_to_all(array, axes, 0, 0, axis_index_groups=groups, tiled=True)  76.8 us
    ppermute x1, starting transfers between devices, per_device(): got = lax.ppermute(sens, 'phys', [(0, 1), (1, 0)])  8.79 us
    pallas_call x7, Pallas kernels, kernel_call(): pl.pallas_call(kernel, name=name, out_shape=[make(shape, jnp.float32) for...  4.67 us
  transfers between devices with their start and end apart: 1, of which 0 were waited for; matrix products, arithmetic and copies ran while one was open for 0% of the time, Pallas kernels for 0%

profile of v9, /device:TPU:1, one launch (start us, length us, event | category | flops | bytes accessed | tf_op | source)
XLA Modules:
  0.0 91.6 jit_solution(5601472183259202679)
XLA Ops:
  1.3 1.9 %predict.1 = (f32[8,16,128]{2,1,0:T(8,128)S(1)}, f32[16,32768]{1,0:T(8,128)S(1)}) custom-call(f32[16,32768]{1,0:T(8,128)} %bitcast.16, f32[256,128]{1,0:T(8,128)} %bitcast.12, f32[1,16]{1,0:T(1,128)} %observed_hbm.1, f32[1,16]{1,0:T(1,128)} %weight_hbm.1, f32[1]{0:T(128)S(6)} %copy.11.scale), custom_call_target="tpu_custom_call" | custom-call | tf_op jit(solution)/shard_map/predict/pallas_call | solution.py:309
  3.1 8.8 %collective-permute-start = (f32[16,32768]{1,0:T(8,128)S(1)}, f32[16,32768]{1,0:T(8,128)S(1)}, u32[]{:S(2)}, u32[]{:S(2)}) collective-permute-start(f32[16,32768]{1,0:T(8,128)S(1)} %get-tuple-element.8.sens), channel_id=1, source_target_pairs={{0,256},{256,0},{1,257},{257,1},{2,258},{258,2},{3,259},{259,3},{4... | collective-permute-start | bytes 6291464 | tf_op jit(solution)/shard_map/ppermute | solution.py:355
  11.9 7.3 %all_to_all.30.parts.stations = f32[8,16,128]{2,1,0:T(8,128)S(1)} all-to-all(f32[8,16,128]{2,1,0:T(8,128)S(1)} %get-tuple-element.7), channel_id=1, replica_groups=mesh['phys'=2,'sta'=64,'cell'=4] {'phys','cell'}, dimensions={0} | all-to-all | bytes 131072 | tf_op jit(solution)/shard_map/all_to_all | solution.py:336
  19.3 0.0 copy-start
  19.3 0.0 collective-permute-done.got
  19.3 0.8 first_terms.1
  20.1 20.0 %all_to_all.31 = f32[64,1,768]{2,1,0:T(1,128)S(1)} all-to-all(f32[64,1,768]{2,1,0:T(1,128)S(1)} %bitcast.10), channel_id=1, replica_groups={{208,192,80,64,144,128,16,0,216,200,88,72,152,136,24,8,240,224,112,96,1..., dimensions={0} | all-to-all | bytes 393216 | tf_op jit(solution)/shard_map/all_to_all | solution.py:336
  40.1 0.1 owner_sum.1
  40.2 8.8 %all_to_all.32.slices = f32[8,8,128]{2,1,0:T(8,128)S(1)} all-to-all(f32[8,8,128]{2,1,0:T(8,128)S(1)} %owner_sum.1), channel_id=1, replica_groups=mesh['phys'=2,'sta'=64,'cell'=4] {'phys','cell'}, dimensions={0} | all-to-all | bytes 65536 | tf_op jit(solution)/shard_map/all_to_all | solution.py:336
  49.0 16.9 %all_to_all.33 = f32[64,1,896]{2,1,0:T(1,128)S(1)} all-to-all(f32[64,1,896]{2,1,0:T(1,128)S(1)} %bitcast.8), channel_id=1, replica_groups={{208,192,80,64,144,128,16,0,216,200,88,72,152,136,24,8,240,224,112,96,1..., dimensions={0} | all-to-all | bytes 458752 | tf_op jit(solution)/shard_map/all_to_all | solution.py:336
  66.0 0.0 copy-done
  66.0 0.6 model.1
  66.6 9.0 %all_to_all.34.parts = f32[8,16,128]{2,1,0:T(8,128)S(1)} all-to-all(f32[8,16,128]{2,1,0:T(8,128)S(1)} %get-tuple-element.9), channel_id=1, replica_groups=mesh['phys'=2,'sta'=64,'cell'=4] {'phys','cell'}, dimensions={0} | all-to-all | bytes 131072 | tf_op jit(solution)/shard_map/all_to_all | solution.py:336
  75.6 0.7 second_terms.1
  76.3 14.7 %all_to_all.35 = f32[64,1,512]{2,1,0:T(1,128)S(1)} all-to-all(f32[64,1,512]{2,1,0:T(1,128)S(1)} %bitcast.14), channel_id=1, replica_groups={{208,192,80,64,144,128,16,0,216,200,88,72,152,136,24,8,240,224,112,96,1..., dimensions={0} | all-to-all | bytes 262144 | tf_op jit(solution)/shard_map/all_to_all | solution.py:336
  91.0 0.6 second_step.1
  (1 shorter events, 0.0 us)
Async XLA Ops:
  3.1 16.1 %collective-permute-start = (f32[16,32768]{1,0:T(8,128)S(1)}, f32[16,32768]{1,0:T(8,128)S(1)}, u32[]{:S(2)}, u32[]{:S(2)}) collective-permute-start(f32[16,32768]{1,0:T(8,128)S(1)} %get-tuple-element.8.sens), channel_id=1, source_target_pairs={{0,256},{256,0},{1,257},{257,1},{2,258},{258,2},{3,259},{259,3},{4... | collective-permute-start | bytes 6291464 | tf_op jit(solution)/shard_map/ppermute | solution.py:355
  19.3 46.7 %copy-start = (f32[32768]{0:T(1024)S(1)}, f32[32768]{0:T(1024)}, u32[]{:S(2)}) copy-start(f32[32768]{0:T(1024)} %param.9) | copy-start | bytes 393220

commit v10 on v9

--- a/solution.py
+++ b/solution.py
@@ -138,12 +138,13 @@
     halves = sens.shape[0] // SUB
     share = rows // 2
     core = lax.axis_index("phys")
-    for place, method in enumerate((core, 1 - core)):
-        station = parts[method * cell_blocks]
+    for slot, method in enumerate((core, 1 - core)):
+        place = (1 - method) * cell_blocks
+        station = parts[place]
         total = station
         for block in range(1, cell_blocks):
-            total = total + parts[method * cell_blocks + block]
-        wide[place], wide[2 + place] = residual_weights(total[:, 0:1] / root_cells, station)
+            total = total + parts[place + block]
+        wide[slot], wide[2 + slot] = residual_weights(total[:, 0:1] / root_cells, station)
 
     def owner_rows(owner):
         columns, gradients = ([], []), []
@@ -270,7 +271,7 @@
     lane = lane_index(total.shape[0])
     for place, method in enumerate((core, 1 - core)):
         predicted = jnp.sum(jnp.where(lane == method, total, 0.0), axis=1, keepdims=True) / root_cells
-        _, wide[place] = residual_weights(predicted, stations[method * cell_blocks])
+        _, wide[place] = residual_weights(predicted, stations[(1 - method) * cell_blocks])
 
     def owner_rows(owner):
         gradients = []
@@ -353,7 +354,8 @@
         spaces=[pltpu.HBM] * 4 + [pltpu.SMEM],
     )
     got = lax.ppermute(sens, "phys", [(0, 1), (1, 0)])
-    first = swap(first, ("phys", "cell"))
+    late_first = [[*range(cell_blocks, peers), *range(cell_blocks)]]
+    first = swap(first, ("phys", "cell"), late_first)
     (terms,) = kernel_call(
         functools.partial(first_terms_kernel, rows, owners, cell_blocks, root_cells),
         "first_terms",

time: 92.1 us -> 91.8 us (level)
  no operation moved by 1% of the time
where the time goes in v10:
time: 91.8 us; the launch traced here: 91.4 us
  blocking collectives  76.6 us (83%)
  starting transfers between devices  8.79 us (10%)
  Pallas kernels  4.67 us (5%)
  between operations  1.32 us (1%)
    all_to_all x6, blocking collectives, swap(): lax.all_to_all(array, axes, 0, 0, axis_index_groups=groups, tiled=True)  76.6 us
    ppermute x1, starting transfers between devices, per_device(): got = lax.ppermute(sens, 'phys', [(0, 1), (1, 0)])  8.79 us
    pallas_call x7, Pallas kernels, kernel_call(): pl.pallas_call(kernel, name=name, out_shape=[make(shape, jnp.float32) for...  4.67 us
  transfers between devices with their start and end apart: 1, of which 0 were waited for; matrix products, arithmetic and copies ran while one was open for 0% of the time, Pallas kernels for 0%

profile of v10, /device:TPU:1, one launch (start us, length us, event | category | flops | bytes accessed | tf_op | source)
XLA Modules:
  0.0 91.4 jit_solution(16250246621884426429)
XLA Ops:
  1.3 1.9 %predict.1 = (f32[8,16,128]{2,1,0:T(8,128)S(1)}, f32[16,32768]{1,0:T(8,128)S(1)}) custom-call(f32[16,32768]{1,0:T(8,128)} %bitcast.16, f32[256,128]{1,0:T(8,128)} %bitcast.12, f32[1,16]{1,0:T(1,128)} %observed_hbm.1, f32[1,16]{1,0:T(1,128)} %weight_hbm.1, f32[1]{0:T(128)S(6)} %copy.11.scale), custom_call_target="tpu_custom_call" | custom-call | tf_op jit(solution)/shard_map/predict/pallas_call | solution.py:310
  3.1 8.8 %collective-permute-start = (f32[16,32768]{1,0:T(8,128)S(1)}, f32[16,32768]{1,0:T(8,128)S(1)}, u32[]{:S(2)}, u32[]{:S(2)}) collective-permute-start(f32[16,32768]{1,0:T(8,128)S(1)} %get-tuple-element.8.sens), channel_id=1, source_target_pairs={{0,256},{256,0},{1,257},{257,1},{2,258},{258,2},{3,259},{259,3},{4... | collective-permute-start | bytes 6291464 | tf_op jit(solution)/shard_map/ppermute | solution.py:356
  11.9 7.5 %all_to_all.30.parts.stations = f32[8,16,128]{2,1,0:T(8,128)S(1)} all-to-all(f32[8,16,128]{2,1,0:T(8,128)S(1)} %get-tuple-element.7), channel_id=1, replica_groups={{256,257,258,259,0,1,2,3},{260,261,262,263,4,5,6,7},{264,265,266,267,8,..., dimensions={0} | all-to-all | bytes 131072 | tf_op jit(solution)/shard_map/all_to_all | solution.py:337
  19.4 0.0 copy-start
  19.4 0.0 collective-permute-done.got
  19.4 0.8 first_terms.1
  20.2 19.6 %all_to_all.31 = f32[64,1,768]{2,1,0:T(1,128)S(1)} all-to-all(f32[64,1,768]{2,1,0:T(1,128)S(1)} %bitcast.10), channel_id=1, replica_groups={{208,192,80,64,144,128,16,0,216,200,88,72,152,136,24,8,240,224,112,96,1..., dimensions={0} | all-to-all | bytes 393216 | tf_op jit(solution)/shard_map/all_to_all | solution.py:337
  39.8 0.1 owner_sum.1
  39.9 8.8 %all_to_all.32.slices = f32[8,8,128]{2,1,0:T(8,128)S(1)} all-to-all(f32[8,8,128]{2,1,0:T(8,128)S(1)} %owner_sum.1), channel_id=1, replica_groups=mesh['phys'=2,'sta'=64,'cell'=4] {'phys','cell'}, dimensions={0} | all-to-all | bytes 65536 | tf_op jit(solution)/shard_map/all_to_all | solution.py:337
  48.8 16.9 %all_to_all.33 = f32[64,1,896]{2,1,0:T(1,128)S(1)} all-to-all(f32[64,1,896]{2,1,0:T(1,128)S(1)} %bitcast.8), channel_id=1, replica_groups={{208,192,80,64,144,128,16,0,216,200,88,72,152,136,24,8,240,224,112,96,1..., dimensions={0} | all-to-all | bytes 458752 | tf_op jit(solution)/shard_map/all_to_all | solution.py:337
  65.7 0.0 copy-done
  65.7 0.6 model.1
  66.3 9.0 %all_to_all.34.parts = f32[8,16,128]{2,1,0:T(8,128)S(1)} all-to-all(f32[8,16,128]{2,1,0:T(8,128)S(1)} %get-tuple-element.9), channel_id=1, replica_groups=mesh['phys'=2,'sta'=64,'cell'=4] {'phys','cell'}, dimensions={0} | all-to-all | bytes 131072 | tf_op jit(solution)/shard_map/all_to_all | solution.py:337
  75.3 0.7 second_terms.1
  76.0 14.7 %all_to_all.35 = f32[64,1,512]{2,1,0:T(1,128)S(1)} all-to-all(f32[64,1,512]{2,1,0:T(1,128)S(1)} %bitcast.14), channel_id=1, replica_groups={{208,192,80,64,144,128,16,0,216,200,88,72,152,136,24,8,240,224,112,96,1..., dimensions={0} | all-to-all | bytes 262144 | tf_op jit(solution)/shard_map/all_to_all | solution.py:337
  90.8 0.6 second_step.1
  (1 shorter events, 0.0 us)
Async XLA Ops:
  3.1 16.3 %collective-permute-start = (f32[16,32768]{1,0:T(8,128)S(1)}, f32[16,32768]{1,0:T(8,128)S(1)}, u32[]{:S(2)}, u32[]{:S(2)}) collective-permute-start(f32[16,32768]{1,0:T(8,128)S(1)} %get-tuple-element.8.sens), channel_id=1, source_target_pairs={{0,256},{256,0},{1,257},{257,1},{2,258},{258,2},{3,259},{259,3},{4... | collective-permute-start | bytes 6291464 | tf_op jit(solution)/shard_map/ppermute | solution.py:356
  19.4 46.3 %copy-start = (f32[32768]{0:T(1024)S(1)}, f32[32768]{0:T(1024)}, u32[]{:S(2)}) copy-start(f32[32768]{0:T(1024)} %param.9) | copy-start | bytes 393220
